TPU v7x, 256 devices: a whole 4x4x8 slice. The times are simulated.
256 devices in a mesh: resp: 8 (over y, z_hi), prompt: 32 (over x, z_lo, core).
Axes of the slice: x: 4, y: 4, z: 8 (z_hi: 2, z_lo: 4; z = z_hi * 4 + z_lo), core: 2. Of those that a mesh axis runs over, the one named last changes fastest.
Arguments:
- prompt_key_matrix: bfloat16 [512, 512], P('prompt'), may hold values from -4 to 4, as said below
- prompt_value_matrix: bfloat16 [512, 512], P('prompt'), may hold values from -15 to 15
- response_queries: bfloat16 [16, 2048, 2560], P('resp', 'prompt'), may hold values from -4 to 4, as said below
- response_cotangent: bfloat16 [16, 2048, 2560], P('resp', 'prompt'), may hold values from -0.08984375 to 0.08984375
- resp_keys: bfloat16 [16, 2048, 512], P('resp', 'prompt'), may hold values from -4 to 4, as said below
- resp_values: bfloat16 [16, 2048, 512], P('resp', 'prompt'), may hold values from -15 to 15
- thresholds: float32 [16, 2048, 20], P('resp', 'prompt'), may hold values from 0.8 to 1.6, as said below
- lengths: int32 [16], P('resp'), may hold values from 1 to 2048, as said below
Outputs:
- grad_queries: bfloat16 [16, 2048, 2560], P('resp', 'prompt')
- grad_resp_keys: bfloat16 [16, 2048, 512], P('resp', 'prompt')
- grad_resp_values: bfloat16 [16, 2048, 512], P('resp', 'prompt')
- grad_prompt_keys: bfloat16 [512, 512], P('prompt')
- grad_prompt_values: bfloat16 [512, 512], P('prompt')
Inputs may be any that keep to these rules, and one draw needn't show every extreme that they name: `prompt_key_matrix`: every entry is a multiple of 1/16. `response_queries`: every entry is a multiple of 1/16. `resp_keys`: every entry is a multiple of 1/16. `thresholds`: each threshold is an odd multiple of 1 / (512 sqrt(128)). `lengths`: in every draw some response has all 2048 positions.
All inputs are finite; a program needn't handle non-finite values.
Results may differ from a plain program's by a relative error of at most 0.024.
Values may be sent and summed in bfloat16 or wider, within the bound.
No kernel may reach another device: no remote copies, remote signals or barrier semaphores. Data moves between devices by JAX's collectives and lax.ppermute only.
A program may use at most 128 MiB of HBM per device.

v0:
```python
import math

import jax
import jax.numpy as jnp
from jax import lax
from jax.sharding import PartitionSpec as P

QUERY_HEADS = 20
KEY_VALUE_HEADS = 4
HEAD_DIMENSION = 128


def head_scores(row_heads, flat_rows):
    head_rows = flat_rows.reshape(flat_rows.shape[0], row_heads.shape[1], row_heads.shape[3])
    return jnp.einsum("rghd,kgd->ghrk", row_heads, head_rows, preferred_element_type=jnp.float32)


def tile_terms(query_part, cot_part, thresh_part, key_block, value_block, allowed, score_scale):
    scores = head_scores(query_part, key_block) * score_scale
    inside = jnp.logical_and(scores > thresh_part, allowed[None, None])
    prob_grad = head_scores(cot_part, value_block)
    return (scores, inside, prob_grad)


def grad_scores(
    query_part, cot_part, thresh_part, mean_part, key_block, value_block, allowed, score_scale
):
    scores, inside, prob_grad = tile_terms(
        query_part, cot_part, thresh_part, key_block, value_block, allowed, score_scale
    )
    dscore = (jnp.where(inside, prob_grad - mean_part, 0.0) * score_scale).astype(jnp.bfloat16)
    weights = jnp.where(inside, scores - thresh_part, 0.0).astype(jnp.bfloat16)
    return (dscore, weights)


def key_terms(query_part, cot_part, dscore, weights):
    key_count = dscore.shape[-1]
    key_grad = jnp.einsum("ghrk,rghd->kgd", dscore, query_part, preferred_element_type=jnp.float32)
    value_grad = jnp.einsum("ghrk,rghd->kgd", weights, cot_part, preferred_element_type=jnp.float32)
    return jnp.concatenate([key_grad.reshape(key_count, -1), value_grad.reshape(key_count, -1)], -1)


def query_terms(dscore, key_block, row_heads):
    head_rows = key_block.reshape(key_block.shape[0], row_heads.shape[1], row_heads.shape[3])
    return jnp.einsum("ghrk,kgd->rghd", dscore, head_rows, preferred_element_type=jnp.float32)


def block_size(total_rows):
    return math.gcd(total_rows, 512)


def split_rows(one_piece, row_start, row_count):
    if row_count <= 512:
        return one_piece(row_start, row_count)
    span_rows = math.gcd(row_count, 512)

    def one_block(block_index):
        return one_piece(block_index * span_rows, span_rows)

    pieces = lax.map(one_block, jnp.arange(row_count // span_rows, dtype=jnp.int32))
    return pieces.reshape(row_count, pieces.shape[-1])


def key_sweep(key_rows, value_rows, block_rows, block_steps, update, initial):

    def advance(block_index, totals):
        offset = block_index * block_rows
        key_block = lax.dynamic_slice_in_dim(key_rows, offset, block_rows, 0)
        value_block = lax.dynamic_slice_in_dim(value_rows, offset, block_rows, 0)
        return update(totals, key_block, value_block, offset)

    return lax.fori_loop(0, block_steps, advance, initial)


def causal_allowed(positions, length, offset, span_rows):
    key_pos = offset + jnp.arange(span_rows, dtype=jnp.int32)
    return (
        (key_pos[None, :] <= positions[:, None])
        & (key_pos[None, :] < length)
        & (positions[:, None] < length)
    )


def local(
    prompt_key_matrix,
    prompt_value_matrix,
    response_queries,
    response_cotangent,
    resp_keys,
    resp_values,
    thresholds,
    lengths,
):
    members = response_queries.shape[0]
    member_places = response_queries.shape[1]
    group_width = QUERY_HEADS // KEY_VALUE_HEADS
    score_scale = HEAD_DIMENSION ** (-0.5)
    block_widths = KEY_VALUE_HEADS * HEAD_DIMENSION
    joined_rows = members * member_places
    prompt_index = lax.axis_index("prompt")
    query_row_set = response_queries.reshape(
        joined_rows, KEY_VALUE_HEADS, group_width, HEAD_DIMENSION
    )
    cotangent_rows = response_cotangent.reshape(
        joined_rows, KEY_VALUE_HEADS, group_width, HEAD_DIMENSION
    )
    support_threshold = jnp.transpose(
        thresholds.reshape(joined_rows, KEY_VALUE_HEADS, group_width), (1, 2, 0)
    )[..., None]
    positions = prompt_index * member_places + jnp.arange(member_places, dtype=jnp.int32)
    row_live = (positions[None, :] < lengths[:, None]).reshape(joined_rows)
    last_end = (prompt_index + 1) * member_places
    prompt_key_rows, prompt_value_rows = (
        lax.all_gather(prompt_key_matrix, "prompt", axis=0, tiled=True),
        lax.all_gather(prompt_value_matrix, "prompt", axis=0, tiled=True),
    )
    resp_key_rows, resp_value_rows = (
        lax.all_gather(resp_keys, "prompt", axis=1, tiled=True),
        lax.all_gather(resp_values, "prompt", axis=1, tiled=True),
    )
    prompt_total = prompt_key_rows.shape[0]
    resp_total = resp_key_rows.shape[1]
    prompt_block = block_size(prompt_total)
    resp_block = block_size(resp_total)

    def prompt_allowed(offset, span_rows):
        return jnp.broadcast_to(row_live[:, None], (joined_rows, span_rows))

    def member_parts(member):
        lower = member * member_places
        upper = lower + member_places
        live_end = jnp.minimum(last_end, lengths[member])

        def allowed_of(offset, span_rows):
            return causal_allowed(positions, lengths[member], offset, span_rows)

        return (lower, upper, live_end, allowed_of)

    def stats_update(query_part, cot_part, thresh_part, allowed_of):

        def update(totals, key_block, value_block, offset):
            count_sum, grad_sum = totals
            allowed = allowed_of(offset, key_block.shape[0])
            scores, inside, prob_grad = tile_terms(
                query_part, cot_part, thresh_part, key_block, value_block, allowed, score_scale
            )
            return (
                count_sum + jnp.sum(inside.astype(jnp.float32), -1),
                grad_sum + jnp.sum(jnp.where(inside, prob_grad, 0.0), -1),
            )

        return update

    blank_statistics = jnp.zeros((KEY_VALUE_HEADS, group_width, joined_rows), jnp.float32)
    counts, grads = key_sweep(
        prompt_key_rows,
        prompt_value_rows,
        prompt_block,
        prompt_total // prompt_block,
        stats_update(query_row_set, cotangent_rows, support_threshold, prompt_allowed),
        (blank_statistics, blank_statistics),
    )
    member_counts = []
    member_grads = []
    for member in range(members):
        lower, upper, live_end, allowed_of = member_parts(member)
        blank_member = jnp.zeros((KEY_VALUE_HEADS, group_width, member_places), jnp.float32)
        found = key_sweep(
            resp_key_rows[member],
            resp_value_rows[member],
            resp_block,
            (live_end + resp_block - 1) // resp_block,
            stats_update(
                query_row_set[lower:upper],
                cotangent_rows[lower:upper],
                support_threshold[:, :, lower:upper],
                allowed_of,
            ),
            (blank_member, blank_member),
        )
        member_counts.append(found[0])
        member_grads.append(found[1])
    counts = counts + jnp.concatenate(member_counts, -1)
    grads = grads + jnp.concatenate(member_grads, -1)
    grad_mean = (grads / jnp.maximum(counts, 1.0))[..., None]

    def query_update(query_part, cot_part, thresh_part, mean_part, allowed_of):

        def update(totals, key_block, value_block, offset):
            allowed = allowed_of(offset, key_block.shape[0])
            dscore, weights = grad_scores(
                query_part,
                cot_part,
                thresh_part,
                mean_part,
                key_block,
                value_block,
                allowed,
                score_scale,
            )
            return totals + query_terms(dscore, key_block, query_part)

        return update

    query_grad = key_sweep(
        prompt_key_rows,
        prompt_value_rows,
        prompt_block,
        prompt_total // prompt_block,
        query_update(query_row_set, cotangent_rows, support_threshold, grad_mean, prompt_allowed),
        jnp.zeros((joined_rows, KEY_VALUE_HEADS, group_width, HEAD_DIMENSION), jnp.float32),
    )
    member_query = []
    for member in range(members):
        lower, upper, live_end, allowed_of = member_parts(member)
        member_query.append(
            key_sweep(
                resp_key_rows[member],
                resp_value_rows[member],
                resp_block,
                (live_end + resp_block - 1) // resp_block,
                query_update(
                    query_row_set[lower:upper],
                    cotangent_rows[lower:upper],
                    support_threshold[:, :, lower:upper],
                    grad_mean[:, :, lower:upper],
                    allowed_of,
                ),
                jnp.zeros(
                    (member_places, KEY_VALUE_HEADS, group_width, HEAD_DIMENSION), jnp.float32
                ),
            )
        )
    query_grad = query_grad + jnp.concatenate(member_query, 0)
    grad_queries = query_grad.reshape(members, member_places, QUERY_HEADS * HEAD_DIMENSION).astype(
        jnp.bfloat16
    )

    def one_piece(offset, span_rows):
        dscore, weights = grad_scores(
            query_row_set,
            cotangent_rows,
            support_threshold,
            grad_mean,
            prompt_key_rows,
            prompt_value_rows,
            prompt_allowed(offset, span_rows),
            score_scale,
        )
        return key_terms(query_row_set, cotangent_rows, dscore, weights)

    prompt_sums = lax.psum_scatter(
        split_rows(one_piece, jnp.int32(0), prompt_key_matrix.shape[0] * lax.axis_size("prompt")),
        "prompt",
        scatter_dimension=0,
        tiled=True,
    )
    prompt_sums = lax.psum(prompt_sums, "resp")
    grad_prompt_keys = prompt_sums[:, :block_widths].astype(jnp.bfloat16)
    grad_prompt_values = prompt_sums[:, block_widths:].astype(jnp.bfloat16)
    row_start = jnp.int32(0)
    outputs = []
    for member in range(members):
        lower, upper, live_end, allowed_of = member_parts(member)

        def one_piece(
            offset,
            span_rows,
            lower=lower,
            upper=upper,
            live_end=live_end,
            allowed_of=allowed_of,
            member=member,
        ):

            def compute():
                key_block = lax.dynamic_slice_in_dim(resp_key_rows[member], offset, span_rows, 0)
                value_block = lax.dynamic_slice_in_dim(
                    resp_value_rows[member], offset, span_rows, 0
                )
                query_part = query_row_set[lower:upper]
                cot_part = cotangent_rows[lower:upper]
                dscore, weights = grad_scores(
                    query_part,
                    cot_part,
                    support_threshold[:, :, lower:upper],
                    grad_mean[:, :, lower:upper],
                    key_block,
                    value_block,
                    allowed_of(offset, span_rows),
                    score_scale,
                )
                return key_terms(query_part, cot_part, dscore, weights)

            def nothing():
                return jnp.zeros((span_rows, 2 * block_widths), jnp.float32)

            return lax.cond(offset < live_end, compute, nothing)

        outputs.append(split_rows(one_piece, row_start, member_places * lax.axis_size("prompt")))
    resp_sums = lax.psum_scatter(
        jnp.concatenate(outputs, -1).astype(jnp.bfloat16), "prompt", scatter_dimension=0, tiled=True
    ).astype(jnp.float32)
    resp_sums = jnp.transpose(
        resp_sums.reshape(member_places, members, 2, block_widths), (1, 0, 2, 3)
    )
    grad_resp_keys = resp_sums[:, :, 0].astype(jnp.bfloat16)
    grad_resp_values = resp_sums[:, :, 1].astype(jnp.bfloat16)
    return (grad_queries, grad_resp_keys, grad_resp_values, grad_prompt_keys, grad_prompt_values)


def solution(mesh):
    placed = (
        P("prompt", None),
        P("prompt", None),
        P("resp", "prompt", None),
        P("resp", "prompt", None),
        P("resp", "prompt", None),
        P("resp", "prompt", None),
        P("resp", "prompt", None),
        P("resp"),
    )
    return jax.shard_map(
        local,
        mesh=mesh,
        in_specs=placed,
        out_specs=(
            P("resp", "prompt", None),
            P("resp", "prompt", None),
            P("resp", "prompt", None),
            P("prompt", None),
            P("prompt", None),
        ),
        check_vma=False,
    )
```

profile of v0, /device:TPU:24, one launch (start us, length us, event | category | flops | bytes accessed | tf_op | source)
XLA Modules:
  0.0 535.6 jit_solution(6128841545272605335)
XLA Ops:
  7.2 1.8 copy.232
  9.0 1.7 copy.234
  10.8 1.3 fusion.136
  13.5 47.7 %all_gather.12 = bf16[512,512]{1,0:T(8,128)(2,1)S(1)} all-gather(bf16[16,512]{1,0:T(8,128)(2,1)} %param.24), channel_id=1, replica_groups=mesh['resp'=8,'prompt'=32] {'prompt'}, dimensions={0}, use_global_device_ids=true | all-gather | bytes 540672 | tf_op jit(solution)/shard_map/all_gather | solution.py:114
  64.3 1.8 reshape.605
  67.5 1.4 slice.141
  70.8 41.4 %all_gather.13 = bf16[512,512]{1,0:T(8,128)(2,1)S(1)} all-gather(bf16[16,512]{1,0:T(8,128)(2,1)S(1)} %copy-done.16), channel_id=1, replica_groups=mesh['resp'=8,'prompt'=32] {'prompt'}, dimensions={0}, use_global_device_ids=true | all-gather | bytes 540672 | tf_op jit(solution)/shard_map/all_gather | solution.py:115
  113.1 1.5 copy.272
  116.0 4.0 fusion.104
  120.0 1.1 fusion.111
  121.1 1.3 copy.274
  122.5 10.0 %fusion.129 = (bf16[1,2048,512]{2,0,1:T(2,128)(2,1)}, bf16[1,2048,512]{2,0,1:T(2,128)(2,1)}) fusion(bf16[2,2048,512]{2,0,1:T(2,128)(2,1)} %all-gather.3.cloned.1.call-done), kind=kLoop, calls=%fused_computation.197 | loop fusion | bytes 8388608 | tf_op jit(solution)/shard_map/slice | solution.py:169
  132.5 10.6 %copy.347 = bf16[1,2048,512]{1,2,0:T(8,128)(2,1)} copy(bf16[1,2048,512]{2,0,1:T(2,128)(2,1)} %get-tuple-element.1168) | data formatting | bytes 4194304 | tf_op jit(solution)/shard_map/squeeze | solution.py:169
  143.1 10.1 %fusion.128 = (bf16[1,2048,512]{2,0,1:T(2,128)(2,1)}, bf16[1,2048,512]{2,0,1:T(2,128)(2,1)}) fusion(bf16[2,2048,512]{2,0,1:T(2,128)(2,1)} %all-gather.5.cloned.1.call-done), kind=kLoop, calls=%fused_computation.196 | loop fusion | bytes 8388608 | tf_op jit(solution)/shard_map/slice | solution.py:170
  153.2 10.6 %copy.348 = bf16[1,2048,512]{1,2,0:T(8,128)(2,1)} copy(bf16[1,2048,512]{2,0,1:T(2,128)(2,1)} %get-tuple-element.1166) | data formatting | bytes 4194304 | tf_op jit(solution)/shard_map/squeeze | solution.py:170
  163.9 4.9 while.82
  165.9 1.3 constant_dynamic-slice_fusion.17
  169.6 9.0 %copy.345 = bf16[1,2048,512]{1,2,0:T(8,128)(2,1)S(1)} copy(bf16[1,2048,512]{2,0,1:T(2,128)(2,1)} %get-tuple-element.1167) | data formatting | bytes 4194304 | tf_op jit(solution)/shard_map/squeeze | solution.py:169
  178.6 10.7 %copy.346 = bf16[1,2048,512]{1,2,0:T(8,128)(2,1)} copy(bf16[1,2048,512]{2,0,1:T(2,128)(2,1)} %get-tuple-element.1165) | data formatting | bytes 4194304 | tf_op jit(solution)/shard_map/squeeze | solution.py:170
  189.2 3.9 while.81
  189.4 1.1 constant_dynamic-slice_fusion.16
  190.6 2.0 convert_reduce_fusion.5
  193.3 5.9 %fusion.124 = f32[4,512,128,1]{1,2,3,0:T(8,128)} fusion(bf16[128,4,5,128]{3,0,2,1:T(8,128)(2,1)S(1)} %copy.270, pred[4,5,128,512]{2,3,1,0:T(32,128)(4,1)} %copy-done.1, f32[4,512,128,5]{2,1,3,0:T(8,128)} %get-tuple-element.1183, f32[4,5,128]{2,1,0:T(8,128)S(1)} %fusion.118), kind=kOutput, calls=%fused_computation.195 | convolution fusion | flops 340787200 | bytes 8267776 | tf_op jit(solution)/shard_map/ghrk,rghd->kgd/dot_general | solution.py:38
  199.2 1.6 copy.273
  200.8 1.5 pad_maximum_fusion.1
  202.6 11.2 %copy.257 = bf16[2,2048,512]{1,2,0:T(8,128)(2,1)} copy(bf16[2,2048,512]{2,0,1:T(2,128)(2,1)} %all-gather.3.cloned.1.call-done) | data formatting | bytes 8388608
  213.8 11.3 %copy.259 = bf16[2,2048,512]{1,2,0:T(8,128)(2,1)} copy(bf16[2,2048,512]{2,0,1:T(2,128)(2,1)} %all-gather.5.cloned.1.call-done) | data formatting | bytes 8388608
  225.2 2.6 broadcast.399.clone2
  227.7 25.3 %while.86 = (s32[]{:T(128)}, bf16[4,512,1024]{2,1,0:T(8,128)(2,1)}, s32[4]{0:T(128)S(1)}, s32[]{:T(128)}, bf16[2,2048,512]{1,2,0:T(8,128)(2,1)}, /*index=5*/bf16...) while((s32[]{:T(128)}, bf16[4,512,1024]{2,1,0:T(8,128)(2,1)}, ...), condition=%wide.region_21.22_spmd.clone, body=%wide.region_18.21_spmd.clone.sunk | while | flops 681805440 | bytes 30845420 | solution.py:60
  229.0 13.5 %conditional.7 = (bf16[1,512,1024]{1,2,0:T(8,128)(2,1)S(1)}) conditional(s32[]{:T(128)} %convert_element_type.117, () %tuple.203, (bf16[2,2048,512]{1,2,0:T(8,128)(2,1)}, s32[]{:T(128)}, bf16[128,4,5,128]{3,0,2,1:T(8,128)(2,1)S(1)}, f32[4,5,128,1]{2,1,0,3:T(8,128)S(1)}, s32[]{:T(128)}, /*index=5*/s32[2]{0:T(128)S(1)}, ...), branch_computations={%region_19.19_spmd, %region_20.20_spmd} | conditional | flops 681805440 | bytes 26650598 | solution.py:298
  229.0 1.7 slice.113
  230.8 1.7 slice.109
  232.5 1.3 constant_dynamic-slice_fusion.2
  236.2 1.7 fusion.48
  238.0 3.2 fusion.47
  241.2 1.3 maximum_bitcast_fusion.1
  248.9 1.1 constant_dynamic-update-slice_fusion.5
  251.9 1.1 constant_dynamic-update-slice_fusion.5
  253.0 2.6 broadcast.399.clone2.1
  255.6 23.5 %while.85 = (s32[]{:T(128)}, bf16[4,512,1024]{2,1,0:T(8,128)(2,1)}, s32[4]{0:T(128)S(1)}, s32[]{:T(128)}, bf16[2,2048,512]{1,2,0:T(8,128)(2,1)}, /*index=5*/bf16...) while((s32[]{:T(128)}, bf16[4,512,1024]{2,1,0:T(8,128)(2,1)}, ...), condition=%wide.region_17.18_spmd.clone, body=%wide.region_14.17_spmd.clone.sunk | while | flops 681805440 | bytes 30845412 | solution.py:60
  256.9 11.8 %conditional.6 = (bf16[1,512,1024]{1,2,0:T(8,128)(2,1)S(1)}) conditional(s32[]{:T(128)} %convert_element_type.116, () %tuple.200, (bf16[2,2048,512]{1,2,0:T(8,128)(2,1)}, s32[]{:T(128)}, bf16[128,4,5,128]{3,0,2,1:T(8,128)(2,1)S(1)}, f32[4,5,128,1]{2,1,0,3:T(8,128)S(1)}, s32[]{:T(128)}, /*index=5*/s32[2]{0:T(128)S(1)}, ...), branch_computations={%region_15.15_spmd, %region_16.16_spmd} | conditional | flops 681805440 | bytes 26650590 | solution.py:298
  256.9 1.7 slice.106
  258.6 1.7 slice.102
  260.4 1.3 constant_dynamic-slice_fusion
  262.4 1.7 fusion.19
  264.1 3.2 fusion.18
  267.4 1.3 maximum_bitcast_fusion
  272.1 1.1 constant_dynamic-update-slice_fusion.4
  278.0 1.1 constant_dynamic-update-slice_fusion.4
  279.1 8.2 %pad_maximum_fusion = bf16[2048,2048]{1,0:T(8,128)(2,1)} fusion(bf16[2048,1024]{1,0:T(8,128)(2,1)} %bitcast.457, bf16[2048,1024]{1,0:T(8,128)(2,1)} %bitcast.458), kind=kLoop, calls=%fused_computation.160 | loop fusion | flops 16777216 | bytes 16777216 | tf_op jit(solution)/shard_map/concatenate | solution.py:302
  288.4 9.1 %while.84 = (s32[]{:T(128)}, f32[64,4,5,128]{3,0,2,1:T(8,128)}, s32[]{:T(128)}, bf16[2048,512]{0,1:T(8,128)(2,1)}, bf16[64,4,5,128]{3,0,2,1:T(8,128)(2,1)}, /*in...) while((s32[]{:T(128)}, f32[64,4,5,128]{3,0,2,1:T(8,128)}, ...), condition=%wide.region_13.14_spmd.clone, body=%wide.region_12.13_spmd.clone.sunk | while | flops 508167872 | bytes 10436455 | solution.py:72
  288.4 2.1 constant_dynamic-slice_fusion.19
  290.4 1.5 fusion.215
  293.9 3.6 fusion.216
  298.4 7.3 %while.83 = (s32[]{:T(128)}, f32[64,4,5,128]{3,0,2,1:T(8,128)}, s32[]{:T(128)}, bf16[2048,512]{0,1:T(8,128)(2,1)}, bf16[64,4,5,128]{3,0,2,1:T(8,128)(2,1)}, /*in...) while((s32[]{:T(128)}, f32[64,4,5,128]{3,0,2,1:T(8,128)}, ...), condition=%wide.region_11.12_spmd.clone, body=%wide.region_10.11_spmd.clone.sunk | while | flops 508167872 | bytes 10436447 | solution.py:72
  298.4 2.1 constant_dynamic-slice_fusion.18
  300.5 1.5 fusion.208
  302.1 3.6 fusion.209
  305.7 4.8 fusion.117
  311.0 1.6 convert_element_type.63
  312.5 51.6 %reduce-scatter.5.cloned.1.call-done = f32[16,1024]{1,0:T(8,128)} async-done(((f32[512,1024]{1,0:T(8,128)}), f32[16,1024]{1,0:T(8,128)}) %reduce-scatter.5.cloned.1.call-update) | async-done | bytes 65552 | tf_op jit(solution)/shard_map/reduce_scatter | solution.py:252
  364.1 52.4 %psum.7 = bf16[16,1024]{1,0:T(8,128)(2,1)S(1)} all-reduce(f32[16,1024]{1,0:T(8,128)} %reduce-scatter.5.cloned.1.call-done), channel_id=1, replica_groups=mesh['resp'=8,'prompt'=32] {'resp'}, use_global_device_ids=true, to_apply=%region_24.25 | all-reduce | flops 16384 | bytes 98304 | tf_op jit(solution)/shard_map/psum | solution.py:258
  417.1 109.6 %reduce-scatter.3.cloned.1.call-done = bf16[64,2048]{1,0:T(8,128)(2,1)} async-done(((bf16[2048,2048]{1,0:T(8,128)(2,1)}), bf16[64,2048]{1,0:T(8,128)(2,1)}) %reduce-scatter.3.cloned.1.call-update) | async-done | bytes 262160 | tf_op jit(solution)/shard_map/reduce_scatter | solution.py:301
  526.7 1.1 reshape.608
  (160 shorter events, 37.8 us)
Async XLA Ops:
  7.2 54.3 %copy-start.9 = (bf16[2,64,2560]{2,1,0:T(8,128)(2,1)S(1)}, bf16[2,64,2560]{2,1,0:T(8,128)(2,1)}, u32[]{:S(2)}) copy-start(bf16[2,64,2560]{2,1,0:T(8,128)(2,1)} %param.26) | copy-start | bytes 1966084
  7.2 115.4 %all-gather.3.cloned.1.call-start = ((), (), s32[]{:S(2)}) async-start(), calls=%async_computation.2 | async-start | bytes 4325376 | tf_op jit(solution)/shard_map/all_gather | solution.py:118
  9.0 134.2 %all-gather.5.cloned.1.call-start = ((), (), s32[]{:S(2)}) async-start(), calls=%async_computation.3 | async-start | bytes 4325376 | tf_op jit(solution)/shard_map/all_gather | solution.py:119
  10.8 353.4 %reduce-scatter.5.cloned.1.call-start = ((), (), s32[]{:S(2)}) async-start(), calls=%async_computation.5 | async-start | bytes 2162688 | tf_op jit(solution)/shard_map/reduce_scatter | solution.py:252
  61.4 53.3 %copy-start.4 = (bf16[512,512]{0,1:T(8,128)(2,1)}, bf16[512,512]{0,1:T(8,128)(2,1)S(1)}, u32[]{:S(2)}) copy-start(bf16[512,512]{0,1:T(8,128)(2,1)S(1)} %copy.226) | copy-start | bytes 1572868
  61.4 2.9 copy-start.15
  61.4 2.9 copy-start.10
  66.9 2.8 copy-start.11
  66.9 3.4 copy-start.14
  67.5 3.3 copy-start.16
  114.6 5.4 %copy-start.6 = (bf16[128,4,5,128]{3,0,2,1:T(8,128)(2,1)}, bf16[128,4,5,128]{3,0,2,1:T(8,128)(2,1)S(1)}, u32[]{:S(2)}) copy-start(bf16[128,4,5,128]{3,0,2,1:T(8,128)(2,1)S(1)} %copy.272) | copy-start | bytes 1966084
  114.7 1.3 copy-start.12
  120.0 1.1 copy-start.1
  153.2 10.7 %copy-start.13 = (bf16[64,4,5,128]{3,0,2,1:T(8,128)(2,1)S(1)}, bf16[64,4,5,128]{3,0,2,1:T(8,128)(2,1)}, u32[]{:S(2)}) copy-start(bf16[64,4,5,128]{3,0,2,1:T(8,128)(2,1)} %copy.243) | copy-start | bytes 983044
  168.8 0.8 copy-start.3
  193.2 6.0 %copy-start = (bf16[2048,512]{0,1:T(8,128)(2,1)}, bf16[2048,512]{0,1:T(8,128)(2,1)S(1)}, u32[]{:S(2)}) copy-start(bf16[2048,512]{0,1:T(8,128)(2,1)S(1)} %get-tuple-element.1905) | copy-start | bytes 6291460
  193.2 6.0 %copy-start.2 = (bf16[64,4,5,128]{3,0,2,1:T(8,128)(2,1)}, bf16[64,4,5,128]{3,0,2,1:T(8,128)(2,1)S(1)}, u32[]{:S(2)}) copy-start(bf16[64,4,5,128]{3,0,2,1:T(8,128)(2,1)S(1)} %get-tuple-element.1907) | copy-start | bytes 983044
  199.1 1.7 copy-start.5
  202.3 324.4 %reduce-scatter.3.cloned.1.call-start = ((), (), s32[]{:S(2)}) async-start(), calls=%async_computation.4 | async-start | bytes 8650752 | tf_op jit(solution)/shard_map/reduce_scatter | solution.py:301
  232.5 3.7 copy-start.7
  260.4 2.0 copy-start.8
Sparse Core Ops, SparseCore 0:
  10.4 66.3 all-gather.2
  79.3 61.9 all-gather.4
  202.4 161.6 reduce-scatter.4
  366.7 159.9 reduce-scatter.2
where the time goes:
time: 538 us; the launch traced here: 536 us
  waiting for transfers between devices  161 us (30%)
  local copies, waits for them, and re-layouts  152 us (28%)
  blocking collectives  141 us (26%)
  matrix products  41.8 us (8%)
  other arithmetic  17.1 us (3%)
  between operations  15.4 us (3%)
  loops' own time  6.01 us (1%)
    reduce_scatter x1, waiting for transfers between devices, local(): lax.psum_scatter(jnp.concatenate(outputs, -1).astype(jnp.bfloat16), 'prom...  110 us
    psum x1, blocking collectives, local(): prompt_sums = lax.psum(prompt_sums, 'resp')  52.4 us
    reduce_scatter x1, waiting for transfers between devices, local(): lax.psum_scatter(split_rows(one_piece, jnp.int32(0), prompt_key_matrix.sh...  51.6 us
    all_gather x1, blocking collectives, local(): lax.all_gather(prompt_key_matrix, 'prompt', axis=0, tiled=True)  47.7 us
    all_gather x1, blocking collectives, local(): lax.all_gather(prompt_value_matrix, 'prompt', axis=0, tiled=True)  41.4 us
    unnamed x38, local copies, waits for them, and re-layouts  29.2 us
    squeeze x2, local copies, waits for them, and re-layouts, local(): resp_value_rows[member]  21.3 us
    squeeze x2, local copies, waits for them, and re-layouts, local(): resp_key_rows[member]  19.6 us
  transfers between devices with their start and end apart: 4, of which 2 were waited for; matrix products, arithmetic and copies ran while one was open for 28% of the time, Pallas kernels for 0%

commit v1 on v0

v1 whole, which is shorter than its diff:
```python
import functools

import jax
import jax.numpy as jnp
from jax import lax
from jax.experimental import pallas as pl
from jax.experimental.pallas import tpu as pltpu
from jax.sharding import Mesh
from jax.sharding import PartitionSpec as P

BF = jnp.bfloat16
F32 = jnp.float32
GROUP = 5
HD = 128
OWN = 64
SPAN = 2 * OWN
ROWS = GROUP * SPAN
WIDE = GROUP * HD
PACKED = 2 * WIDE + HD
PROMPT = 512
OWN_PROMPT = 16
KEYS = PROMPT + 2048
ROOT = HD**0.5
NT = (((1,), (1,)), ((), ()))
NN = (((1,), (0,)), ((), ()))
TN = (((0,), (0,)), ((), ()))


def call(body, out_shape, count, scratch=(), limit=None, name=None):
    vm = pl.BlockSpec(memory_space=pltpu.VMEM)
    return pl.pallas_call(
        body,
        out_shape=out_shape,
        in_specs=[pl.BlockSpec(memory_space=pltpu.SMEM)] + [vm] * count,
        out_specs=jax.tree.map(lambda _: vm, out_shape),
        scratch_shapes=scratch,
        compiler_params=pltpu.CompilerParams(vmem_limit_bytes=limit),
        name=name,
    )


def pack_keys_kernel(where, k_ref, v_ref, pk_ref, pv_ref, own_ref, swap_ref):
    x, core = where[0], where[2]
    for s in range(4):
        head = lax.rem(x + s, 4)
        cols = pl.ds(pl.multiple_of(head * HD, HD), HD)
        for out, member in ((own_ref, core), (swap_ref, 1 - core)):
            out[s, 0:OWN, 0:HD] = k_ref[member, :, cols]
            out[s, 0:OWN, HD:] = v_ref[member, :, cols]
            out[s, OWN:, 0:HD] = pk_ref[:, cols]
            out[s, OWN:, HD:] = pv_ref[:, cols]


def pack_rows_kernel(where, q_ref, c_ref, t_ref, *outs):
    x, core = where[0], where[2]
    for s in range(4):
        head = lax.rem(x + s, 4)
        cols = pl.ds(pl.multiple_of(head * WIDE, HD), WIDE)
        for out, member in ((outs[s], core), (outs[4 + s], 1 - core)):
            out[:, 0:WIDE] = q_ref[member, :, cols]
            out[:, WIDE : 2 * WIDE] = c_ref[member, :, cols]
            left = t_ref[member, head]
            for part in range(3):
                piece = left.astype(BF)
                out[:, 2 * WIDE + part * GROUP : 2 * WIDE + (part + 1) * GROUP] = piece
                left = left - piece.astype(F32)
            out[:, 2 * WIDE + 3 * GROUP :] = jnp.zeros((OWN, HD - 3 * GROUP), BF)


def attend_kernel(step, where, *refs):
    own, par, kvs = refs[0:4], refs[4:8], refs[8:12]
    keep, other, grads, prompt_grads = refs[12:16], refs[16:20], refs[20:24], refs[24:28]
    k_all, v_all, qc_all, t_all, q_st, c_st, prob, grad, dk, dv, dq_t, dq_all = refs[28:]
    x, z, core, length = where[0], where[1], where[2], where[3]
    sides = (core, 1 - core)

    def key_places(j):
        zs = lax.rem(z + 4 - j, 4)
        for s in range(4):
            xs = lax.rem(x + 4 - s, 4)
            for side in range(2):
                at = pl.multiple_of(PROMPT + 512 * xs + SPAN * zs + OWN * sides[side], OWN)
                yield s, side, at

    for j in range(4):
        for s, side, at in key_places(j):
            row = s * 160 + side * 80
            k_all[pl.ds(at, OWN)] = kvs[j][row : row + OWN, 0:HD]
            v_all[pl.ds(at, OWN)] = kvs[j][row : row + OWN, HD:]
            slot = j * 128 + s * 32 + side * 16
            k_all[slot : slot + 16] = kvs[j][row + OWN : row + 80, 0:HD]
            v_all[slot : slot + 16] = kvs[j][row + OWN : row + 80, HD:]
    for s in range(4):
        xs = lax.rem(x + 4 - s, 4)
        for side, ref in ((0, own[s]), (1, par[s])):
            qc_all[xs, pl.ds(pl.multiple_of(OWN * sides[side], OWN), OWN)] = ref[...]
    dk[...] = jnp.zeros_like(dk)
    dv[...] = jnp.zeros_like(dv)
    lane = lax.broadcasted_iota(jnp.int32, (1, SPAN), 1)
    sub = lax.broadcasted_iota(jnp.int32, (SPAN, SPAN), 0)
    col = lax.broadcasted_iota(jnp.int32, (SPAN, SPAN), 1)

    def block(b, carry):
        start = b * 512 + z * SPAN

        @pl.when(start >= length)
        def _():
            dq_all[b] = jnp.zeros((SPAN, WIDE), BF)

        @pl.when(start < length)
        def _():
            for h in range(GROUP):
                q_st[h * SPAN : (h + 1) * SPAN] = qc_all[b, :, h * HD : (h + 1) * HD]
                c_st[h * SPAN : (h + 1) * SPAN] = qc_all[b, :, WIDE + h * HD : WIDE + (h + 1) * HD]
            pieces = qc_all[b, :, 2 * WIDE :].astype(F32).T
            t_all[...] = (
                pieces[0:GROUP] + pieces[GROUP : 2 * GROUP] + pieces[2 * GROUP : 3 * GROUP]
            ) * ROOT
            live_row = start + lane < length
            thr = jnp.concatenate(
                [jnp.where(live_row, t_all[h : h + 1], 1e30) for h in range(GROUP)], 1
            )

            def first(k0, count, bar, totals):
                over = (
                    lax.dot_general(
                        k_all[pl.ds(k0, count)], q_st[...], NT, preferred_element_type=F32
                    )
                    - bar
                )
                weight = jnp.maximum(over, 0.0).astype(BF)
                prob[pl.ds(k0, count)] = weight
                pg = lax.dot_general(
                    v_all[pl.ds(k0, count)], c_st[...], NT, preferred_element_type=F32
                )
                grad[pl.ds(k0, count)] = pg
                live = over > 0.0
                num, tot = totals
                num = num + jnp.sum(jnp.where(live, 1.0, 0.0).reshape(count // 8, 8, ROWS), 0)
                tot = tot + jnp.sum(jnp.where(live, pg, 0.0).reshape(count // 8, 8, ROWS), 0)
                dv[pl.ds(k0, count)] += lax.dot_general(
                    weight, c_st[...], NN, preferred_element_type=F32
                )
                return num, tot

            def main(i, totals):
                return first(pl.multiple_of(i * step, step), step, thr, totals)

            base = PROMPT + b * 512

            def tail(i, totals):
                barred = jnp.where(sub + i * SPAN <= col + z * SPAN, 0.0, 1e30)
                bar = thr + jnp.concatenate([barred] * GROUP, 1)
                return first(pl.multiple_of(base + i * SPAN, SPAN), SPAN, bar, totals)

            zero = jnp.zeros((8, ROWS), F32)
            steps = (1 + b) * (512 // step)
            totals = lax.fori_loop(0, steps, main, (zero, zero))
            num, tot = lax.fori_loop(0, z + 1, tail, totals)
            mean = jnp.sum(tot, 0, keepdims=True) / jnp.maximum(
                jnp.sum(num, 0, keepdims=True), 1.0
            )
            dq_t[...] = jnp.zeros_like(dq_t)

            def second(k0, count):
                centred = (grad[pl.ds(k0, count)] - mean).astype(BF)
                ds = jnp.where(prob[pl.ds(k0, count)] > 0, centred, jnp.zeros((), BF))
                dk[pl.ds(k0, count)] += lax.dot_general(
                    ds, q_st[...], NN, preferred_element_type=F32
                )
                dq_t[...] += lax.dot_general(
                    k_all[pl.ds(k0, count)], ds, TN, preferred_element_type=F32
                )

            def main2(i, carry):
                second(pl.multiple_of(i * step, step), step)
                return carry

            def tail2(i, carry):
                second(pl.multiple_of(base + i * SPAN, SPAN), SPAN)
                return carry

            lax.fori_loop(0, steps, main2, 0)
            lax.fori_loop(0, z + 1, tail2, 0)
            for h in range(GROUP):
                dq_all[b, :, h * HD : (h + 1) * HD] = (
                    dq_t[:, h * SPAN : (h + 1) * SPAN].T * (1.0 / ROOT)
                ).astype(BF)

        return carry

    lax.fori_loop(0, 4, block, 0)
    for s in range(4):
        to = lax.rem(x + s, 4)
        for side, ref in ((0, keep[s]), (1, other[s])):
            ref[...] = dq_all[to, pl.ds(pl.multiple_of(OWN * sides[side], OWN), OWN)]
    for j in range(4):
        for part, total in ((0, dk), (1, dv)):
            cols = slice(part * HD, (part + 1) * HD)
            prompt_grads[j][:, cols] = (total[j * 128 : (j + 1) * 128] * (1.0 / ROOT)).astype(BF)
            for s, side, at in key_places(j):
                row = s * SPAN + side * OWN
                grads[j][row : row + OWN, cols] = (total[pl.ds(at, OWN)] * (1.0 / ROOT)).astype(BF)


def unpack_rows_kernel(where, *refs):
    x, core = where[0], where[2]
    out = refs[8]
    for s in range(4):
        head = lax.rem(x + 4 - s, 4)
        cols = pl.ds(pl.multiple_of(head * WIDE, HD), WIDE)
        out[core, :, cols] = refs[s][...]
        out[1 - core, :, cols] = refs[4 + s][...]


def unpack_keys_kernel(where, *refs):
    x, core = where[0], where[2]
    mine, swapped = refs[0:4], refs[4]
    out_k, out_v = refs[5:]
    for s in range(4):
        head = lax.rem(x + s, 4)
        cols = pl.ds(pl.multiple_of(head * HD, HD), HD)
        out_k[core, :, cols] = mine[s][0:OWN, 0:HD]
        out_v[core, :, cols] = mine[s][0:OWN, HD:]
        out_k[1 - core, :, cols] = swapped[s, :, 0:HD]
        out_v[1 - core, :, cols] = swapped[s, :, HD:]


def unpack_prompt_kernel(where, *refs):
    x = where[0]
    mine, swapped = refs[0:4], refs[4]
    out = refs[5]
    for s in range(4):
        head = lax.rem(x + s, 4)
        total = mine[s][0:OWN_PROMPT].astype(F32) + swapped[s].astype(F32)
        for part in range(2):
            cols = pl.ds(pl.multiple_of(part * 4 * HD + head * HD, HD), HD)
            out[:, cols] = total[:, part * HD : (part + 1) * HD]


def shift(values, axis, by):
    by %= 4
    if by == 0:
        return values
    return lax.ppermute(values, axis, [(i, (i + by) % 4) for i in range(4)])


def swap(values):
    return lax.ppermute(values, "core", [(0, 1), (1, 0)])


def shift_swap(values, by):
    pairs = [(2 * i + c, 2 * ((i + by) % 4) + 1 - c) for i in range(4) for c in range(2)]
    return lax.ppermute(values, ("x", "core"), pairs)


def local(
    prompt_key_matrix,
    prompt_value_matrix,
    response_queries,
    response_cotangent,
    resp_keys,
    resp_values,
    thresholds,
    lengths,
):
    x, z, core = lax.axis_index("x"), lax.axis_index("z"), lax.axis_index("core")
    length = lax.dynamic_index_in_dim(lengths, core, 0, keepdims=False)
    where = jnp.stack([x, z, core, length]).astype(jnp.int32)
    shape = jax.ShapeDtypeStruct
    kv_own, kv_swap = call(
        pack_keys_kernel, [shape((4, 80, 2 * HD), BF)] * 2, 4, name="pack_keys"
    )(where, resp_keys, resp_values, prompt_key_matrix, prompt_value_matrix)
    kv_other = swap(kv_swap)
    chip = jnp.concatenate([kv_own, kv_other], 1)
    payload = jnp.concatenate([shift(chip[s], "x", s) for s in range(4)], 0)
    kvs = [shift(payload, "z", j) for j in range(4)]

    thresh = jnp.transpose(thresholds.reshape(2, OWN, 4, GROUP), (0, 2, 1, 3))
    rows = call(pack_rows_kernel, [shape((OWN, PACKED), BF)] * 8, 3, name="pack_rows")(
        where, response_queries, response_cotangent, thresh
    )
    own = [shift(rows[s], "x", s) for s in range(4)]
    par = [shift_swap(rows[4 + s], s) for s in range(4)]

    outs = call(
        functools.partial(attend_kernel, 512),
        [shape((OWN, WIDE), BF)] * 8 + [shape((512, 2 * HD), BF)] * 4 + [shape((128, 2 * HD), BF)] * 4,
        12,
        [
            pltpu.VMEM((KEYS, HD), BF),
            pltpu.VMEM((KEYS, HD), BF),
            pltpu.VMEM((4, SPAN, PACKED), BF),
            pltpu.VMEM((GROUP, SPAN), F32),
            pltpu.VMEM((ROWS, HD), BF),
            pltpu.VMEM((ROWS, HD), BF),
            pltpu.VMEM((KEYS, ROWS), BF),
            pltpu.VMEM((KEYS, ROWS), F32),
            pltpu.VMEM((KEYS, HD), F32),
            pltpu.VMEM((KEYS, HD), F32),
            pltpu.VMEM((HD, ROWS), F32),
            pltpu.VMEM((4, SPAN, WIDE), BF),
        ],
        48 * 1024 * 1024,
        "attend",
    )(where, *own, *par, *kvs)
    keep, other, grads, prompt_grads = outs[0:4], outs[4:8], outs[8:12], outs[12:16]

    def summed(parts):
        got = [shift(parts[j], "z", -j).astype(F32) for j in range(4)]
        return (got[0] + got[1] + got[2] + got[3]).astype(BF)

    prompt_sum = summed(prompt_grads)
    prompt_back = [shift(prompt_sum[32 * s : 32 * s + 32], "x", -s) for s in range(4)]
    prompt_swapped = swap(jnp.stack([p[OWN_PROMPT:] for p in prompt_back]))
    prompt_total = call(unpack_prompt_kernel, shape((OWN_PROMPT, 8 * HD), F32), 5, name="unpack_prompt")(
        where, *prompt_back, prompt_swapped
    )
    for mask in (1, 2, 4):
        prompt_total = prompt_total + lax.ppermute(
            prompt_total, "resp", [(i, i ^ mask) for i in range(8)]
        )
    grad_prompt_keys = prompt_total[:, : 4 * HD].astype(BF)
    grad_prompt_values = prompt_total[:, 4 * HD :].astype(BF)

    back_own = [shift(keep[s], "x", s) for s in range(4)]
    back_par = [shift_swap(other[s], s) for s in range(4)]
    grad_queries = call(unpack_rows_kernel, shape((2, OWN, 4 * WIDE), BF), 8, name="unpack_rows")(
        where, *back_own, *back_par
    )

    key_sum = summed(grads)
    key_back = [shift(key_sum[SPAN * s : SPAN * (s + 1)], "x", -s) for s in range(4)]
    key_swapped = swap(jnp.stack([p[OWN:] for p in key_back]))
    grad_resp_keys, grad_resp_values = call(
        unpack_keys_kernel, [shape((2, OWN, 4 * HD), BF)] * 2, 5, name="unpack_keys"
    )(where, *key_back, key_swapped)
    return (grad_queries, grad_resp_keys, grad_resp_values, grad_prompt_keys, grad_prompt_values)


def solution(mesh):
    fine = Mesh(mesh.devices.reshape(8, 4, 4, 2), ("resp", "x", "z", "core"))
    line = ("x", "z", "core")
    by_row = P("resp", line, None)
    return jax.shard_map(
        local,
        mesh=fine,
        in_specs=(P(line, None), P(line, None), by_row, by_row, by_row, by_row, by_row, P("resp")),
        out_specs=(by_row, by_row, by_row, P(line, None), P(line, None)),
        check_vma=False,
    )
```

time: 538 us -> 143 us (0.27)
  local copies, waits for them, and re-layouts: 152 us -> 8.31 us
  blocking collectives: 141 us -> 0 us
  waiting for transfers between devices: 161 us -> 49.3 us
  starting transfers between devices: 0.38 us -> 58.8 us
  matrix products: 41.8 us -> 0 us
  Pallas kernels: 0 us -> 20.9 us
  other arithmetic: 17.1 us -> 2.37 us
  between operations: 15.4 us -> 0.93 us
  loops' own time: 6.01 us -> 0 us
    reduce_scatter x2 -> x0, waiting for transfers between devices: 161 us -> none  [the longest x1 110 us: local(): lax.psum_scatter(jnp.concatenate(outputs, -1).astype(jnp.bfloat16), 'prom...]
    all_gather x2 -> x0, blocking collectives: 89.1 us -> none  [the longest x1 47.7 us: local(): lax.all_gather(prompt_key_matrix, 'prompt', axis=0, tiled=True)]
    ppermute x0 -> x38, starting transfers between devices: none -> 58.8 us  [the longest x24 42.3 us: shift(): return lax.ppermute(values, axis, [(i, (i + by) % 4) for i in range(4)])]
    psum x1 -> x0, blocking collectives: 52.4 us -> none  [local(): prompt_sums = lax.psum(prompt_sums, 'resp')]
    ppermute x0 -> x38, waiting for transfers between devices: none -> 49.3 us  [the longest x24 24.8 us: shift(): return lax.ppermute(values, axis, [(i, (i + by) % 4) for i in range(4)])]
    dot_general x19 -> x0, matrix products: 41.8 us -> none  [the longest x10 12.9 us: head_scores(): jnp.einsum('rghd,kgd->ghrk', row_heads, head_rows, preferred_element_type...]
    squeeze x4 -> x1, local copies, waits for them, and re-layouts: 40.9 us -> 0.02 us  [local(): payload = jnp.concatenate([shift(chip[s], 'x', s) for s in range(4)], 0)]
    slice x20 -> x3, local copies, waits for them, and re-layouts: 35.2 us -> 1.86 us  [the longest x1 0.63 us: local(): key_sum[SPAN * s:SPAN * (s + 1)]]
  transfers between devices with their start and end apart: 4 -> 38, of which waited for: 2 -> 12; matrix products, arithmetic and copies ran while one was open for 28% -> 3% of each run, Pallas kernels for 0% -> 4%
where the time goes in v1:
time: 143 us; the launch traced here: 141 us
  starting transfers between devices  58.8 us (41%)
  waiting for transfers between devices  49.3 us (34%)
  Pallas kernels  20.9 us (15%)
  local copies, waits for them, and re-layouts  8.31 us (6%)
  other arithmetic  2.37 us (2%)
    ppermute x24, starting transfers between devices, shift(): return lax.ppermute(values, axis, [(i, (i + by) % 4) for i in range(4)])  42.3 us
    ppermute x24, waiting for transfers between devices, shift(): return lax.ppermute(values, axis, [(i, (i + by) % 4) for i in range(4)])  24.8 us
    ppermute x3, waiting for transfers between devices, local(): lax.ppermute(prompt_total, 'resp', [(i, i ^ mask) for i in range(8)])  12.8 us
    ppermute x3, starting transfers between devices, local(): lax.ppermute(prompt_total, 'resp', [(i, i ^ mask) for i in range(8)])  11.2 us
    pallas_call x1, Pallas kernels, local(): call(functools.partial(attend_kernel, 512), [shape((OWN, WIDE), BF)] * 8...  11.1 us
    ppermute x8, waiting for transfers between devices, shift_swap(): return lax.ppermute(values, ('x', 'core'), pairs)  10.3 us
    unnamed x45, local copies, waits for them, and re-layouts  4.95 us
    ppermute x3, starting transfers between devices, swap(): return lax.ppermute(values, 'core', [(0, 1), (1, 0)])  2.94 us
  transfers between devices with their start and end apart: 38, of which 12 were waited for; matrix products, arithmetic and copies ran while one was open for 3% of the time, Pallas kernels for 4%

profile of v1, /device:TPU:24, one launch (start us, length us, event | category | flops | bytes accessed | tf_op | source)
XLA Modules:
  0.0 140.6 jit_solution(13703900637598415589)
XLA Ops:
  0.6 0.6 copy-done.21
  1.3 0.6 dynamic_slice.4
  1.9 1.3 pad_add_fusion.where
  3.1 1.8 %pack_keys.1 = (bf16[4,80,256]{2,1,0:T(8,128)(2,1)}, bf16[4,80,256]{2,1,0:T(8,128)(2,1)}) custom-call(s32[4]{0:T(128)} %pad_add_fusion.where, bf16[2,64,512]{2,1,0:T(8,128)(2,1)} %k_ref.1, bf16[2,64,512]{2,1,0:T(8,128)(2,1)} %v_ref.1, bf16[16,512]{1,0:T(8,128)(2,1)} %pk_ref.1, bf16[16,512]{1,0:T(8,128)(2,1)} %pv_ref.1), custom_call_target="tpu_custom_call" | custom-call | tf_op jit(solution)/shard_map/pack_keys/pallas_call | solution.py:271
  4.9 0.9 constant_dynamic-update-slice_fusion.1
  5.8 0.7 collective-permute-done.7
  6.6 2.8 %collective-permute-start.10 = (bf16[160,256]{1,0:T(8,128)(2,1)S(1)}, bf16[160,256]{1,0:T(8,128)(2,1)S(1)}, u32[]{:S(2)}, u32[]{:S(2)}) collective-permute-start(bf16[160,256]{1,0:T(8,128)(2,1)S(1)} %get-tuple-element.62), channel_id=1, source_target_pairs={{0,24},{8,0},{16,8},{24,16},{1,25},{9,1},{17,9},{25,17},{2,26},{10... | collective-permute-start | bytes 245768 | tf_op jit(solution)/shard_map/ppermute | solution.py:245
  9.4 0.8 collective-permute-start.9
  10.2 0.9 collective-permute-start.8
  11.1 0.9 copy.13
  12.0 2.6 %pack_rows.1 = (bf16[64,1408]{1,0:T(8,128)(2,1)}, bf16[64,1408]{1,0:T(8,128)(2,1)}, bf16[64,1408]{1,0:T(8,128)(2,1)}, bf16[64,1408]{1,0:T(8,128)(2,1)}, bf16[64,...) custom-call(s32[4]{0:T(128)} %pad_add_fusion.where, ...), custom_call_target="tpu_custom_call" | custom-call | tf_op jit(solution)/shard_map/pack_rows/pallas_call | solution.py:280
  14.6 1.8 %collective-permute-start = (bf16[64,1408]{1,0:T(8,128)(2,1)}, bf16[64,1408]{1,0:T(8,128)(2,1)S(1)}, u32[]{:S(2)}, u32[]{:S(2)}) collective-permute-start(bf16[64,1408]{1,0:T(8,128)(2,1)} %get-tuple-element.34), channel_id=1, source_target_pairs={{0,8},{8,16},{16,24},{24,0},{1,9},{9,17},{17,25},{25,1},{2,10},{10... | collective-permute-start | bytes 540680 | tf_op jit(solution)/shard_map/ppermute | solution.py:245
  16.4 2.0 %collective-permute-start.1 = (bf16[64,1408]{1,0:T(8,128)(2,1)}, bf16[64,1408]{1,0:T(8,128)(2,1)S(1)}, u32[]{:S(2)}, u32[]{:S(2)}) collective-permute-start(bf16[64,1408]{1,0:T(8,128)(2,1)} %get-tuple-element.35), channel_id=1, source_target_pairs={{0,16},{8,24},{16,0},{24,8},{1,17},{9,25},{17,1},{25,9},{2,18},{10... | collective-permute-start | bytes 540680 | tf_op jit(solution)/shard_map/ppermute | solution.py:245
  18.4 0.7 collective-permute-start.2
  19.1 1.4 %collective-permute-start.4 = (bf16[64,1408]{1,0:T(8,128)(2,1)}, bf16[64,1408]{1,0:T(8,128)(2,1)S(1)}, u32[]{:S(2)}, u32[]{:S(2)}) collective-permute-start(bf16[64,1408]{1,0:T(8,128)(2,1)} %get-tuple-element.38), channel_id=1, source_target_pairs={{0,9},{1,8},{8,17},{9,16},{16,25},{17,24},{24,1},{25,0},{2,11},{3,... | collective-permute-start | bytes 540680 | tf_op jit(solution)/shard_map/ppermute | solution.py:254
  20.6 2.3 %collective-permute-done.refs_1_ = bf16[64,1408]{1,0:T(8,128)(2,1)S(1)} collective-permute-done((bf16[64,1408]{1,0:T(8,128)(2,1)}, bf16[64,1408]{1,0:T(8,128)(2,1)S(1)}, u32[]{:S(2)}, u32[]{:S(2)}) %collective-permute-start) | collective-permute-done | bytes 180256 | tf_op jit(solution)/shard_map/ppermute | solution.py:245
  22.9 4.6 %collective-permute-start.13 = (bf16[640,256]{1,0:T(8,128)(2,1)S(1)}, bf16[640,256]{1,0:T(8,128)(2,1)S(1)}, u32[]{:S(2)}, u32[]{:S(2)}) collective-permute-start(bf16[640,256]{1,0:T(8,128)(2,1)S(1)} %pad_maximum_fusion.refs_8_), channel_id=1, source_target_pairs={{0,6},{2,0},{4,2},{6,4},{1,7},{3,1},{5,3},{7,5},{8,14},{10,8},{12,... | collective-permute-start | bytes 983048 | tf_op jit(solution)/shard_map/ppermute | solution.py:245
  27.5 0.4 collective-permute-done.1.refs_2_
  27.9 3.3 %collective-permute-start.12 = (bf16[640,256]{1,0:T(8,128)(2,1)S(1)}, bf16[640,256]{1,0:T(8,128)(2,1)S(1)}, u32[]{:S(2)}, u32[]{:S(2)}) collective-permute-start(bf16[640,256]{1,0:T(8,128)(2,1)S(1)} %pad_maximum_fusion.refs_8_), channel_id=1, source_target_pairs={{0,4},{2,6},{4,0},{6,2},{1,5},{3,7},{5,1},{7,3},{8,12},{10,14},{12... | collective-permute-start | bytes 983048 | tf_op jit(solution)/shard_map/ppermute | solution.py:245
  31.2 1.9 %collective-permute-start.11 = (bf16[640,256]{1,0:T(8,128)(2,1)S(1)}, bf16[640,256]{1,0:T(8,128)(2,1)S(1)}, u32[]{:S(2)}, u32[]{:S(2)}) collective-permute-start(bf16[640,256]{1,0:T(8,128)(2,1)S(1)} %pad_maximum_fusion.refs_8_), channel_id=1, source_target_pairs={{0,2},{2,4},{4,6},{6,0},{1,3},{3,5},{5,7},{7,1},{8,10},{10,12},{12... | collective-permute-start | bytes 983048 | tf_op jit(solution)/shard_map/ppermute | solution.py:245
  33.2 0.4 collective-permute-start.6
  33.5 6.5 %collective-permute-done.5.refs_6_ = bf16[64,1408]{1,0:T(8,128)(2,1)S(1)} collective-permute-done((bf16[64,1408]{1,0:T(8,128)(2,1)S(1)}, bf16[64,1408]{1,0:T(8,128)(2,1)S(1)}, u32[]{:S(2)}, u32[]{:S(2)}) %collective-permute-start.5) | collective-permute-done | bytes 180256 | tf_op jit(solution)/shard_map/ppermute | solution.py:254
  40.1 12.9 %collective-permute-done.12.refs_10_ = bf16[640,256]{1,0:T(8,128)(2,1)S(1)} collective-permute-done((bf16[640,256]{1,0:T(8,128)(2,1)S(1)}, bf16[640,256]{1,0:T(8,128)(2,1)S(1)}, u32[]{:S(2)}, u32[]{:S(2)}) %collective-permute-start.12) | collective-permute-done | bytes 327712 | tf_op jit(solution)/shard_map/ppermute | solution.py:245
  53.0 11.1 %attend.1 = (bf16[64,640]{1,0:T(8,128)(2,1)S(1)}, bf16[64,640]{1,0:T(8,128)(2,1)S(1)}, bf16[64,640]{1,0:T(8,128)(2,1)S(1)}, bf16[64,640]{1,0:T(8,128)(2,1)S(1)},...) custom-call(s32[4]{0:T(128)S(1)} %copy-done.2, ...), custom_call_target="tpu_custom_call" | custom-call | tf_op jit(solution)/shard_map/attend/pallas_call | solution.py:286
  64.2 7.7 %collective-permute-start.29 = (bf16[128,256]{1,0:T(8,128)(2,1)S(1)}, bf16[128,256]{1,0:T(8,128)(2,1)S(1)}, u32[]{:S(2)}, u32[]{:S(2)}) collective-permute-start(bf16[128,256]{1,0:T(8,128)(2,1)S(1)} %get-tuple-element.59), channel_id=1, source_target_pairs={{0,4},{2,6},{4,0},{6,2},{1,5},{3,7},{5,1},{7,3},{8,12},{10,14},{12... | collective-permute-start | bytes 196616 | tf_op jit(solution)/shard_map/ppermute | solution.py:245
  71.9 1.9 %collective-permute-start.30 = (bf16[128,256]{1,0:T(8,128)(2,1)S(1)}, bf16[128,256]{1,0:T(8,128)(2,1)S(1)}, u32[]{:S(2)}, u32[]{:S(2)}) collective-permute-start(bf16[128,256]{1,0:T(8,128)(2,1)S(1)} %get-tuple-element.60), channel_id=1, source_target_pairs={{0,2},{2,4},{4,6},{6,0},{1,3},{3,5},{5,7},{7,1},{8,10},{10,12},{12... | collective-permute-start | bytes 196616 | tf_op jit(solution)/shard_map/ppermute | solution.py:245
  73.9 0.4 collective-permute-start.14
  74.2 2.5 %collective-permute-start.15 = (bf16[64,640]{1,0:T(8,128)(2,1)S(1)}, bf16[64,640]{1,0:T(8,128)(2,1)S(1)}, u32[]{:S(2)}, u32[]{:S(2)}) collective-permute-start(bf16[64,640]{1,0:T(8,128)(2,1)S(1)} %get-tuple-element.45), channel_id=1, source_target_pairs={{0,16},{8,24},{16,0},{24,8},{1,17},{9,25},{17,1},{25,9},{2,18},{10... | collective-permute-start | bytes 245768 | tf_op jit(solution)/shard_map/ppermute | solution.py:245
  76.7 1.3 collective-permute-start.16
  78.1 0.6 fusion.1
  78.7 0.7 collective-permute-start.33
  79.4 2.1 %collective-permute-start.32 = (bf16[32,256]{1,0:T(8,128)(2,1)S(1)}, bf16[32,256]{1,0:T(8,128)(2,1)S(1)}, u32[]{:S(2)}, u32[]{:S(2)}) collective-permute-start(bf16[32,256]{1,0:T(8,128)(2,1)S(1)} %get-tuple-element.70), channel_id=1, source_target_pairs={{0,16},{8,24},{16,0},{24,8},{1,17},{9,25},{17,1},{25,9},{2,18},{10... | collective-permute-start | bytes 49160 | tf_op jit(solution)/shard_map/ppermute | solution.py:245
  81.5 2.2 %collective-permute-done.33.refs_3_ = bf16[32,256]{1,0:T(8,128)(2,1)S(1)} collective-permute-done((bf16[32,256]{1,0:T(8,128)(2,1)S(1)}, bf16[32,256]{1,0:T(8,128)(2,1)S(1)}, u32[]{:S(2)}, u32[]{:S(2)}) %collective-permute-start.33) | collective-permute-done | bytes 16416 | tf_op jit(solution)/shard_map/ppermute | solution.py:245
  83.7 0.2 collective-permute-start.31
  83.9 1.0 collective-permute-done.32.refs_2_
  84.8 2.6 %collective-permute-done.31.refs_1_ = bf16[32,256]{1,0:T(8,128)(2,1)S(1)} collective-permute-done((bf16[32,256]{1,0:T(8,128)(2,1)S(1)}, bf16[32,256]{1,0:T(8,128)(2,1)S(1)}, u32[]{:S(2)}, u32[]{:S(2)}) %collective-permute-start.31) | collective-permute-done | bytes 16416 | tf_op jit(solution)/shard_map/ppermute | solution.py:245
  87.4 0.6 copy-done.16
  88.0 2.9 %collective-permute-start.34 = (bf16[4,16,256]{2,1,0:T(8,128)(2,1)S(1)}, bf16[4,16,256]{2,1,0:T(8,128)(2,1)S(1)}, u32[]{:S(2)}, u32[]{:S(2)}) collective-permute-start(bf16[4,16,256]{2,1,0:T(8,128)(2,1)S(1)} %pad_maximum_fusion.2), channel_id=1, source_target_pairs={{0,1},{1,0},{2,3},{3,2},{4,5},{5,4},{6,7},{7,6},{8,9},{9,8},{10,11... | collective-permute-start | bytes 98312 | tf_op jit(solution)/shard_map/ppermute | solution.py:249
  91.0 1.9 %collective-permute-start.21 = (bf16[512,256]{1,0:T(8,128)(2,1)S(1)}, bf16[512,256]{1,0:T(8,128)(2,1)S(1)}, u32[]{:S(2)}, u32[]{:S(2)}) collective-permute-start(bf16[512,256]{1,0:T(8,128)(2,1)S(1)} %get-tuple-element.52), channel_id=1, source_target_pairs={{0,6},{2,0},{4,2},{6,4},{1,7},{3,1},{5,3},{7,5},{8,14},{10,8},{12,... | collective-permute-start | bytes 786440 | tf_op jit(solution)/shard_map/ppermute | solution.py:245
  92.9 1.2 collective-permute-start.23
  94.1 0.3 collective-permute-start.18
  94.4 0.3 copy-done.17
  94.7 1.5 %unpack_prompt.1 = f32[16,1024]{1,0:T(8,128)} custom-call(s32[4]{0:T(128)} %pad_add_fusion.where, bf16[32,256]{1,0:T(8,128)(2,1)} %get-tuple-element.72.refs_0_, bf16[32,256]{1,0:T(8,128)(2,1)} %copy-done.16, bf16[32,256]{1,0:T(8,128)(2,1)} %copy-done.15, bf16[32,256]{1,0:T(8,128)(2,1)} %copy-done.14, bf16[4,16,256]{2,1,0:T(8,128)(2,1)} %copy-done.17), custom_call_target="tpu_custom_call" | custom-call | tf_op jit(solution)/shard_map/unpack_prompt/pallas_call | solution.py:316
  96.2 0.1 collective-permute-start.35
  96.3 3.8 %collective-permute-done.18.refs_5_ = bf16[64,640]{1,0:T(8,128)(2,1)S(1)} collective-permute-done((bf16[64,640]{1,0:T(8,128)(2,1)S(1)}, bf16[64,640]{1,0:T(8,128)(2,1)S(1)}, u32[]{:S(2)}, u32[]{:S(2)}) %collective-permute-start.18) | collective-permute-done | bytes 81952 | tf_op jit(solution)/shard_map/ppermute | solution.py:254
  100.1 12.8 %collective-permute-done.35 = f32[16,1024]{1,0:T(8,128)S(1)} collective-permute-done((f32[16,1024]{1,0:T(8,128)}, f32[16,1024]{1,0:T(8,128)S(1)}, u32[]{:S(2)}, u32[]{:S(2)}) %collective-permute-start.35) | collective-permute-done | bytes 65568 | tf_op jit(solution)/shard_map/ppermute | solution.py:320
  112.8 0.3 collective-permute-start.20
  113.1 0.9 add.38
  114.0 7.1 %collective-permute-start.36 = (f32[16,1024]{1,0:T(8,128)S(1)}, f32[16,1024]{1,0:T(8,128)S(1)}, u32[]{:S(2)}, u32[]{:S(2)}) collective-permute-start(f32[16,1024]{1,0:T(8,128)S(1)} %add.38), channel_id=1, source_target_pairs={{0,64},{32,96},{64,0},{96,32},{128,192},{160,224},{192,128},{224,1... | collective-permute-start | bytes 196616 | tf_op jit(solution)/shard_map/ppermute | solution.py:320
  121.1 0.6 copy-done.13
  121.7 2.1 %unpack_rows.1 = bf16[2,64,2560]{2,1,0:T(8,128)(2,1)} custom-call(s32[4]{0:T(128)} %pad_add_fusion.where, bf16[64,640]{1,0:T(8,128)(2,1)} %copy-done.1, bf16[64,640]{1,0:T(8,128)(2,1)} %copy-done.7, bf16[64,640]{1,0:T(8,128)(2,1)} %copy-done.8, bf16[64,640]{1,0:T(8,128)(2,1)} %copy-done.9, bf16[64,640]{1,0:T(8,128)(2,1)} %copy-done.10, ...), custom_call_target="tpu_custom_call" | custom-call | tf_op jit(solution)/shard_map/unpack_rows/pallas_call | solution.py:328
  123.9 4.0 %collective-permute-start.37 = (f32[16,1024]{1,0:T(8,128)S(1)}, f32[16,1024]{1,0:T(8,128)S(1)}, u32[]{:S(2)}, u32[]{:S(2)}) collective-permute-start(f32[16,1024]{1,0:T(8,128)S(1)} %add.39), channel_id=1, source_target_pairs={{0,128},{32,160},{64,192},{96,224},{128,0},{160,32},{192,64},{224,... | collective-permute-start | bytes 196616 | tf_op jit(solution)/shard_map/ppermute | solution.py:320
  127.9 0.1 add_convert_fusion
  128.1 0.6 fusion
  128.7 0.8 collective-permute-start.26
  129.5 1.4 collective-permute-start.25
  130.9 1.3 collective-permute-start.24
  132.2 3.4 %collective-permute-done.26.refs_3_ = bf16[128,256]{1,0:T(8,128)(2,1)S(1)} collective-permute-done((bf16[128,256]{1,0:T(8,128)(2,1)S(1)}, bf16[128,256]{1,0:T(8,128)(2,1)S(1)}, u32[]{:S(2)}, u32[]{:S(2)}) %collective-permute-start.26) | collective-permute-done | bytes 65568 | tf_op jit(solution)/shard_map/ppermute | solution.py:245
  135.6 0.6 copy-done.3
  136.3 0.6 copy-done.5
  136.8 0.6 fusion.2
  137.5 0.7 collective-permute-done.27.refs_4_
  138.2 0.6 copy-done.6
  138.8 1.8 %unpack_keys.1 = (bf16[2,64,512]{2,1,0:T(8,128)(2,1)}, bf16[2,64,512]{2,1,0:T(8,128)(2,1)}) custom-call(s32[4]{0:T(128)} %pad_add_fusion.where, bf16[128,256]{1,0:T(8,128)(2,1)} %get-tuple-element.68.refs_0_, bf16[128,256]{1,0:T(8,128)(2,1)} %copy-done.5, bf16[128,256]{1,0:T(8,128)(2,1)} %copy-done.4, bf16[128,256]{1,0:T(8,128)(2,1)} %copy-done.3, ...), custom_call_target="tpu_custom_call" | custom-call | tf_op jit(solution)/shard_map/unpack_keys/pallas_call | solution.py:335
  (87 shorter events, 0.5 us)
Async XLA Ops:
  0.6 0.7 copy-start.21
  4.9 1.6 %collective-permute-start.7 = (bf16[4,80,256]{2,1,0:T(8,128)(2,1)}, bf16[4,80,256]{2,1,0:T(8,128)(2,1)S(1)}, u32[]{:S(2)}, u32[]{:S(2)}) collective-permute-start(bf16[4,80,256]{2,1,0:T(8,128)(2,1)} %get-tuple-element.42), channel_id=1, source_target_pairs={{0,1},{1,0},{2,3},{3,2},{4,5},{5,4},{6,7},{7,6},{8,9},{9,8},{10,11... | collective-permute-start | bytes 491528 | tf_op jit(solution)/shard_map/ppermute | solution.py:249
  6.5 4.6 %copy-start.18 = (f32[2,64,20]{1,0,2:T(2,128)S(1)}, f32[2,64,20]{1,0,2:T(2,128)}, u32[]{:S(2)}) copy-start(f32[2,64,20]{1,0,2:T(2,128)} %param.14) | copy-start | bytes 30724
  6.6 11.8 %collective-permute-start.10 = (bf16[160,256]{1,0:T(8,128)(2,1)S(1)}, bf16[160,256]{1,0:T(8,128)(2,1)S(1)}, u32[]{:S(2)}, u32[]{:S(2)}) collective-permute-start(bf16[160,256]{1,0:T(8,128)(2,1)S(1)} %get-tuple-element.62), channel_id=1, source_target_pairs={{0,24},{8,0},{16,8},{24,16},{1,25},{9,1},{17,9},{25,17},{2,26},{10... | collective-permute-start | bytes 245768 | tf_op jit(solution)/shard_map/ppermute | solution.py:245
  9.4 9.7 %collective-permute-start.9 = (bf16[160,256]{1,0:T(8,128)(2,1)S(1)}, bf16[160,256]{1,0:T(8,128)(2,1)S(1)}, u32[]{:S(2)}, u32[]{:S(2)}) collective-permute-start(bf16[160,256]{1,0:T(8,128)(2,1)S(1)} %get-tuple-element.63), channel_id=1, source_target_pairs={{0,16},{8,24},{16,0},{24,8},{1,17},{9,25},{17,1},{25,9},{2,18},{10... | collective-permute-start | bytes 245768 | tf_op jit(solution)/shard_map/ppermute | solution.py:245
  10.2 8.9 %collective-permute-start.8 = (bf16[160,256]{1,0:T(8,128)(2,1)S(1)}, bf16[160,256]{1,0:T(8,128)(2,1)S(1)}, u32[]{:S(2)}, u32[]{:S(2)}) collective-permute-start(bf16[160,256]{1,0:T(8,128)(2,1)S(1)} %get-tuple-element.64), channel_id=1, source_target_pairs={{0,8},{8,16},{16,24},{24,0},{1,9},{9,17},{17,25},{25,1},{2,10},{10... | collective-permute-start | bytes 245768 | tf_op jit(solution)/shard_map/ppermute | solution.py:245
  14.6 8.3 %collective-permute-start = (bf16[64,1408]{1,0:T(8,128)(2,1)}, bf16[64,1408]{1,0:T(8,128)(2,1)S(1)}, u32[]{:S(2)}, u32[]{:S(2)}) collective-permute-start(bf16[64,1408]{1,0:T(8,128)(2,1)} %get-tuple-element.34), channel_id=1, source_target_pairs={{0,8},{8,16},{16,24},{24,0},{1,9},{9,17},{17,25},{25,1},{2,10},{10... | collective-permute-start | bytes 540680 | tf_op jit(solution)/shard_map/ppermute | solution.py:245
  16.4 11.6 %collective-permute-start.1 = (bf16[64,1408]{1,0:T(8,128)(2,1)}, bf16[64,1408]{1,0:T(8,128)(2,1)S(1)}, u32[]{:S(2)}, u32[]{:S(2)}) collective-permute-start(bf16[64,1408]{1,0:T(8,128)(2,1)} %get-tuple-element.35), channel_id=1, source_target_pairs={{0,16},{8,24},{16,0},{24,8},{1,17},{9,25},{17,1},{25,9},{2,18},{10... | collective-permute-start | bytes 540680 | tf_op jit(solution)/shard_map/ppermute | solution.py:245
  18.4 12.8 %collective-permute-start.2 = (bf16[64,1408]{1,0:T(8,128)(2,1)}, bf16[64,1408]{1,0:T(8,128)(2,1)S(1)}, u32[]{:S(2)}, u32[]{:S(2)}) collective-permute-start(bf16[64,1408]{1,0:T(8,128)(2,1)} %get-tuple-element.36), channel_id=1, source_target_pairs={{0,24},{8,0},{16,8},{24,16},{1,25},{9,1},{17,9},{25,17},{2,26},{10... | collective-permute-start | bytes 540680 | tf_op jit(solution)/shard_map/ppermute | solution.py:245
  19.1 14.0 %collective-permute-start.3 = (bf16[64,1408]{1,0:T(8,128)(2,1)}, bf16[64,1408]{1,0:T(8,128)(2,1)S(1)}, u32[]{:S(2)}, u32[]{:S(2)}) collective-permute-start(bf16[64,1408]{1,0:T(8,128)(2,1)} %get-tuple-element.37), channel_id=1, source_target_pairs={{0,1},{1,0},{8,9},{9,8},{16,17},{17,16},{24,25},{25,24},{2,3},{3,2... | collective-permute-start | bytes 540680 | tf_op jit(solution)/shard_map/ppermute | solution.py:254
  19.1 14.0 %collective-permute-start.4 = (bf16[64,1408]{1,0:T(8,128)(2,1)}, bf16[64,1408]{1,0:T(8,128)(2,1)S(1)}, u32[]{:S(2)}, u32[]{:S(2)}) collective-permute-start(bf16[64,1408]{1,0:T(8,128)(2,1)} %get-tuple-element.38), channel_id=1, source_target_pairs={{0,9},{1,8},{8,17},{9,16},{16,25},{17,24},{24,1},{25,0},{2,11},{3,... | collective-permute-start | bytes 540680 | tf_op jit(solution)/shard_map/ppermute | solution.py:254
  20.6 12.6 %copy-start.20 = (bf16[64,1408]{1,0:T(8,128)(2,1)S(1)}, bf16[64,1408]{1,0:T(8,128)(2,1)}, u32[]{:S(2)}) copy-start(bf16[64,1408]{1,0:T(8,128)(2,1)} %get-tuple-element.39) | copy-start | bytes 540676
  20.6 12.6 %copy-start.19 = (bf16[64,1408]{1,0:T(8,128)(2,1)S(1)}, bf16[64,1408]{1,0:T(8,128)(2,1)}, u32[]{:S(2)}) copy-start(bf16[64,1408]{1,0:T(8,128)(2,1)} %get-tuple-element.40) | copy-start | bytes 540676
  20.6 32.4 %copy-start = (bf16[64,1408]{1,0:T(8,128)(2,1)S(1)}, bf16[64,1408]{1,0:T(8,128)(2,1)}, u32[]{:S(2)}) copy-start(bf16[64,1408]{1,0:T(8,128)(2,1)} %get-tuple-element.33.refs_0_) | copy-start | bytes 540676
  22.9 17.1 %collective-permute-start.13 = (bf16[640,256]{1,0:T(8,128)(2,1)S(1)}, bf16[640,256]{1,0:T(8,128)(2,1)S(1)}, u32[]{:S(2)}, u32[]{:S(2)}) collective-permute-start(bf16[640,256]{1,0:T(8,128)(2,1)S(1)} %pad_maximum_fusion.refs_8_), channel_id=1, source_target_pairs={{0,6},{2,0},{4,2},{6,4},{1,7},{3,1},{5,3},{7,5},{8,14},{10,8},{12,... | collective-permute-start | bytes 983048 | tf_op jit(solution)/shard_map/ppermute | solution.py:245
  27.9 25.0 %collective-permute-start.12 = (bf16[640,256]{1,0:T(8,128)(2,1)S(1)}, bf16[640,256]{1,0:T(8,128)(2,1)S(1)}, u32[]{:S(2)}, u32[]{:S(2)}) collective-permute-start(bf16[640,256]{1,0:T(8,128)(2,1)S(1)} %pad_maximum_fusion.refs_8_), channel_id=1, source_target_pairs={{0,4},{2,6},{4,0},{6,2},{1,5},{3,7},{5,1},{7,3},{8,12},{10,14},{12... | collective-permute-start | bytes 983048 | tf_op jit(solution)/shard_map/ppermute | solution.py:245
  31.2 21.8 %collective-permute-start.11 = (bf16[640,256]{1,0:T(8,128)(2,1)S(1)}, bf16[640,256]{1,0:T(8,128)(2,1)S(1)}, u32[]{:S(2)}, u32[]{:S(2)}) collective-permute-start(bf16[640,256]{1,0:T(8,128)(2,1)S(1)} %pad_maximum_fusion.refs_8_), channel_id=1, source_target_pairs={{0,2},{2,4},{4,6},{6,0},{1,3},{3,5},{5,7},{7,1},{8,10},{10,12},{12... | collective-permute-start | bytes 983048 | tf_op jit(solution)/shard_map/ppermute | solution.py:245
  33.1 6.9 %collective-permute-start.5 = (bf16[64,1408]{1,0:T(8,128)(2,1)S(1)}, bf16[64,1408]{1,0:T(8,128)(2,1)S(1)}, u32[]{:S(2)}, u32[]{:S(2)}) collective-permute-start(bf16[64,1408]{1,0:T(8,128)(2,1)S(1)} %copy-done.20), channel_id=1, source_target_pairs={{0,17},{1,16},{8,25},{9,24},{16,1},{17,0},{24,9},{25,8},{2,19},{3,... | collective-permute-start | bytes 540680 | tf_op jit(solution)/shard_map/ppermute | solution.py:254
  33.2 19.8 %copy-start.2 = (s32[4]{0:T(128)S(1)}, s32[4]{0:T(128)}, u32[]{:S(2)}) copy-start(s32[4]{0:T(128)} %pad_add_fusion.where) | copy-start | bytes 52
  33.2 6.9 %collective-permute-start.6 = (bf16[64,1408]{1,0:T(8,128)(2,1)S(1)}, bf16[64,1408]{1,0:T(8,128)(2,1)S(1)}, u32[]{:S(2)}, u32[]{:S(2)}) collective-permute-start(bf16[64,1408]{1,0:T(8,128)(2,1)S(1)} %copy-done.19), channel_id=1, source_target_pairs={{0,25},{1,24},{8,1},{9,0},{16,9},{17,8},{24,17},{25,16},{2,27},{3,... | collective-permute-start | bytes 540680 | tf_op jit(solution)/shard_map/ppermute | solution.py:254
  64.1 13.9 %copy-start.1 = (bf16[64,640]{1,0:T(8,128)(2,1)}, bf16[64,640]{1,0:T(8,128)(2,1)S(1)}, u32[]{:S(2)}) copy-start(bf16[64,640]{1,0:T(8,128)(2,1)S(1)} %get-tuple-element.43.refs_0_) | copy-start | bytes 245764
  64.1 12.6 %collective-permute-start.28 = (bf16[128,256]{1,0:T(8,128)(2,1)S(1)}, bf16[128,256]{1,0:T(8,128)(2,1)S(1)}, u32[]{:S(2)}, u32[]{:S(2)}) collective-permute-start(bf16[128,256]{1,0:T(8,128)(2,1)S(1)} %get-tuple-element.58), channel_id=1, source_target_pairs={{0,6},{2,0},{4,2},{6,4},{1,7},{3,1},{5,3},{7,5},{8,14},{10,8},{12,... | collective-permute-start | bytes 196616 | tf_op jit(solution)/shard_map/ppermute | solution.py:245
  64.2 13.8 %collective-permute-start.29 = (bf16[128,256]{1,0:T(8,128)(2,1)S(1)}, bf16[128,256]{1,0:T(8,128)(2,1)S(1)}, u32[]{:S(2)}, u32[]{:S(2)}) collective-permute-start(bf16[128,256]{1,0:T(8,128)(2,1)S(1)} %get-tuple-element.59), channel_id=1, source_target_pairs={{0,4},{2,6},{4,0},{6,2},{1,5},{3,7},{5,1},{7,3},{8,12},{10,14},{12... | collective-permute-start | bytes 196616 | tf_op jit(solution)/shard_map/ppermute | solution.py:245
  71.9 6.1 %collective-permute-start.30 = (bf16[128,256]{1,0:T(8,128)(2,1)S(1)}, bf16[128,256]{1,0:T(8,128)(2,1)S(1)}, u32[]{:S(2)}, u32[]{:S(2)}) collective-permute-start(bf16[128,256]{1,0:T(8,128)(2,1)S(1)} %get-tuple-element.60), channel_id=1, source_target_pairs={{0,2},{2,4},{4,6},{6,0},{1,3},{3,5},{5,7},{7,1},{8,10},{10,12},{12... | collective-permute-start | bytes 196616 | tf_op jit(solution)/shard_map/ppermute | solution.py:245
  73.9 19.0 %collective-permute-start.14 = (bf16[64,640]{1,0:T(8,128)(2,1)S(1)}, bf16[64,640]{1,0:T(8,128)(2,1)S(1)}, u32[]{:S(2)}, u32[]{:S(2)}) collective-permute-start(bf16[64,640]{1,0:T(8,128)(2,1)S(1)} %get-tuple-element.44), channel_id=1, source_target_pairs={{0,8},{8,16},{16,24},{24,0},{1,9},{9,17},{17,25},{25,1},{2,10},{10... | collective-permute-start | bytes 245768 | tf_op jit(solution)/shard_map/ppermute | solution.py:245
  74.2 18.7 %collective-permute-start.15 = (bf16[64,640]{1,0:T(8,128)(2,1)S(1)}, bf16[64,640]{1,0:T(8,128)(2,1)S(1)}, u32[]{:S(2)}, u32[]{:S(2)}) collective-permute-start(bf16[64,640]{1,0:T(8,128)(2,1)S(1)} %get-tuple-element.45), channel_id=1, source_target_pairs={{0,16},{8,24},{16,0},{24,8},{1,17},{9,25},{17,1},{25,9},{2,18},{10... | collective-permute-start | bytes 245768 | tf_op jit(solution)/shard_map/ppermute | solution.py:245
  76.7 17.4 %collective-permute-start.16 = (bf16[64,640]{1,0:T(8,128)(2,1)S(1)}, bf16[64,640]{1,0:T(8,128)(2,1)S(1)}, u32[]{:S(2)}, u32[]{:S(2)}) collective-permute-start(bf16[64,640]{1,0:T(8,128)(2,1)S(1)} %get-tuple-element.46), channel_id=1, source_target_pairs={{0,24},{8,0},{16,8},{24,16},{1,25},{9,1},{17,9},{25,17},{2,26},{10... | collective-permute-start | bytes 245768 | tf_op jit(solution)/shard_map/ppermute | solution.py:245
  78.7 5.0 %collective-permute-start.33 = (bf16[32,256]{1,0:T(8,128)(2,1)S(1)}, bf16[32,256]{1,0:T(8,128)(2,1)S(1)}, u32[]{:S(2)}, u32[]{:S(2)}) collective-permute-start(bf16[32,256]{1,0:T(8,128)(2,1)S(1)} %get-tuple-element.69), channel_id=1, source_target_pairs={{0,8},{8,16},{16,24},{24,0},{1,9},{9,17},{17,25},{25,1},{2,10},{10... | collective-permute-start | bytes 49160 | tf_op jit(solution)/shard_map/ppermute | solution.py:245
  79.4 5.5 %collective-permute-start.32 = (bf16[32,256]{1,0:T(8,128)(2,1)S(1)}, bf16[32,256]{1,0:T(8,128)(2,1)S(1)}, u32[]{:S(2)}, u32[]{:S(2)}) collective-permute-start(bf16[32,256]{1,0:T(8,128)(2,1)S(1)} %get-tuple-element.70), channel_id=1, source_target_pairs={{0,16},{8,24},{16,0},{24,8},{1,17},{9,25},{17,1},{25,9},{2,18},{10... | collective-permute-start | bytes 49160 | tf_op jit(solution)/shard_map/ppermute | solution.py:245
  83.7 1.2 copy-start.14
  83.7 3.7 %collective-permute-start.31 = (bf16[32,256]{1,0:T(8,128)(2,1)S(1)}, bf16[32,256]{1,0:T(8,128)(2,1)S(1)}, u32[]{:S(2)}, u32[]{:S(2)}) collective-permute-start(bf16[32,256]{1,0:T(8,128)(2,1)S(1)} %get-tuple-element.71), channel_id=1, source_target_pairs={{0,24},{8,0},{16,8},{24,16},{1,25},{9,1},{17,9},{25,17},{2,26},{10... | collective-permute-start | bytes 49160 | tf_op jit(solution)/shard_map/ppermute | solution.py:245
  84.8 2.6 %copy-start.15 = (bf16[32,256]{1,0:T(8,128)(2,1)}, bf16[32,256]{1,0:T(8,128)(2,1)S(1)}, u32[]{:S(2)}) copy-start(bf16[32,256]{1,0:T(8,128)(2,1)S(1)} %collective-permute-done.32.refs_2_) | copy-start | bytes 49156
  87.4 0.6 copy-start.16
  88.0 6.1 %collective-permute-start.34 = (bf16[4,16,256]{2,1,0:T(8,128)(2,1)S(1)}, bf16[4,16,256]{2,1,0:T(8,128)(2,1)S(1)}, u32[]{:S(2)}, u32[]{:S(2)}) collective-permute-start(bf16[4,16,256]{2,1,0:T(8,128)(2,1)S(1)} %pad_maximum_fusion.2), channel_id=1, source_target_pairs={{0,1},{1,0},{2,3},{3,2},{4,5},{5,4},{6,7},{7,6},{8,9},{9,8},{10,11... | collective-permute-start | bytes 98312 | tf_op jit(solution)/shard_map/ppermute | solution.py:249
  91.0 36.9 %collective-permute-start.21 = (bf16[512,256]{1,0:T(8,128)(2,1)S(1)}, bf16[512,256]{1,0:T(8,128)(2,1)S(1)}, u32[]{:S(2)}, u32[]{:S(2)}) collective-permute-start(bf16[512,256]{1,0:T(8,128)(2,1)S(1)} %get-tuple-element.52), channel_id=1, source_target_pairs={{0,6},{2,0},{4,2},{6,4},{1,7},{3,1},{5,3},{7,5},{8,14},{10,8},{12,... | collective-permute-start | bytes 786440 | tf_op jit(solution)/shard_map/ppermute | solution.py:245
  92.9 3.3 %copy-start.7 = (bf16[64,640]{1,0:T(8,128)(2,1)}, bf16[64,640]{1,0:T(8,128)(2,1)S(1)}, u32[]{:S(2)}) copy-start(bf16[64,640]{1,0:T(8,128)(2,1)S(1)} %collective-permute-done.14.refs_1_) | copy-start | bytes 245764
  92.9 35.0 %collective-permute-start.22 = (bf16[512,256]{1,0:T(8,128)(2,1)S(1)}, bf16[512,256]{1,0:T(8,128)(2,1)S(1)}, u32[]{:S(2)}, u32[]{:S(2)}) collective-permute-start(bf16[512,256]{1,0:T(8,128)(2,1)S(1)} %get-tuple-element.53), channel_id=1, source_target_pairs={{0,4},{2,6},{4,0},{6,2},{1,5},{3,7},{5,1},{7,3},{8,12},{10,14},{12... | collective-permute-start | bytes 786440 | tf_op jit(solution)/shard_map/ppermute | solution.py:245
  92.9 3.3 %copy-start.8 = (bf16[64,640]{1,0:T(8,128)(2,1)}, bf16[64,640]{1,0:T(8,128)(2,1)S(1)}, u32[]{:S(2)}) copy-start(bf16[64,640]{1,0:T(8,128)(2,1)S(1)} %collective-permute-done.15.refs_2_) | copy-start | bytes 245764
  92.9 35.0 %collective-permute-start.23 = (bf16[512,256]{1,0:T(8,128)(2,1)S(1)}, bf16[512,256]{1,0:T(8,128)(2,1)S(1)}, u32[]{:S(2)}, u32[]{:S(2)}) collective-permute-start(bf16[512,256]{1,0:T(8,128)(2,1)S(1)} %get-tuple-element.54), channel_id=1, source_target_pairs={{0,2},{2,4},{4,6},{6,0},{1,3},{3,5},{5,7},{7,1},{8,10},{10,12},{12... | collective-permute-start | bytes 786440 | tf_op jit(solution)/shard_map/ppermute | solution.py:245
  94.1 27.0 %copy-start.9 = (bf16[64,640]{1,0:T(8,128)(2,1)}, bf16[64,640]{1,0:T(8,128)(2,1)S(1)}, u32[]{:S(2)}) copy-start(bf16[64,640]{1,0:T(8,128)(2,1)S(1)} %collective-permute-done.16.refs_3_) | copy-start | bytes 245764
  94.1 2.1 %collective-permute-start.17 = (bf16[64,640]{1,0:T(8,128)(2,1)S(1)}, bf16[64,640]{1,0:T(8,128)(2,1)S(1)}, u32[]{:S(2)}, u32[]{:S(2)}) collective-permute-start(bf16[64,640]{1,0:T(8,128)(2,1)S(1)} %get-tuple-element.47), channel_id=1, source_target_pairs={{0,1},{1,0},{8,9},{9,8},{16,17},{17,16},{24,25},{25,24},{2,3},{3,2... | collective-permute-start | bytes 245768 | tf_op jit(solution)/shard_map/ppermute | solution.py:254
  94.1 0.6 copy-start.17
  94.1 6.0 %collective-permute-start.18 = (bf16[64,640]{1,0:T(8,128)(2,1)S(1)}, bf16[64,640]{1,0:T(8,128)(2,1)S(1)}, u32[]{:S(2)}, u32[]{:S(2)}) collective-permute-start(bf16[64,640]{1,0:T(8,128)(2,1)S(1)} %get-tuple-element.48), channel_id=1, source_target_pairs={{0,9},{1,8},{8,17},{9,16},{16,25},{17,24},{24,1},{25,0},{2,11},{3,... | collective-permute-start | bytes 245768 | tf_op jit(solution)/shard_map/ppermute | solution.py:254
  96.2 17.8 %copy-start.10 = (bf16[64,640]{1,0:T(8,128)(2,1)}, bf16[64,640]{1,0:T(8,128)(2,1)S(1)}, u32[]{:S(2)}) copy-start(bf16[64,640]{1,0:T(8,128)(2,1)S(1)} %collective-permute-done.17.refs_4_) | copy-start | bytes 245764
  96.2 16.6 %collective-permute-start.35 = (f32[16,1024]{1,0:T(8,128)}, f32[16,1024]{1,0:T(8,128)S(1)}, u32[]{:S(2)}, u32[]{:S(2)}) collective-permute-start(f32[16,1024]{1,0:T(8,128)} %unpack_prompt.1), channel_id=1, source_target_pairs={{0,32},{32,0},{64,96},{96,64},{128,160},{160,128},{192,224},{224,1... | collective-permute-start | bytes 196616 | tf_op jit(solution)/shard_map/ppermute | solution.py:320
  100.1 21.0 %copy-start.11 = (bf16[64,640]{1,0:T(8,128)(2,1)}, bf16[64,640]{1,0:T(8,128)(2,1)S(1)}, u32[]{:S(2)}) copy-start(bf16[64,640]{1,0:T(8,128)(2,1)S(1)} %collective-permute-done.18.refs_5_) | copy-start | bytes 245764
  100.1 13.9 %collective-permute-start.19 = (bf16[64,640]{1,0:T(8,128)(2,1)S(1)}, bf16[64,640]{1,0:T(8,128)(2,1)S(1)}, u32[]{:S(2)}, u32[]{:S(2)}) collective-permute-start(bf16[64,640]{1,0:T(8,128)(2,1)S(1)} %get-tuple-element.49), channel_id=1, source_target_pairs={{0,17},{1,16},{8,25},{9,24},{16,1},{17,0},{24,9},{25,8},{2,19},{3,... | collective-permute-start | bytes 245768 | tf_op jit(solution)/shard_map/ppermute | solution.py:254
  112.8 8.3 %collective-permute-start.20 = (bf16[64,640]{1,0:T(8,128)(2,1)S(1)}, bf16[64,640]{1,0:T(8,128)(2,1)S(1)}, u32[]{:S(2)}, u32[]{:S(2)}) collective-permute-start(bf16[64,640]{1,0:T(8,128)(2,1)S(1)} %get-tuple-element.50), channel_id=1, source_target_pairs={{0,25},{1,24},{8,1},{9,0},{16,9},{17,8},{24,17},{25,16},{2,27},{3,... | collective-permute-start | bytes 245768 | tf_op jit(solution)/shard_map/ppermute | solution.py:254
  114.0 7.1 %copy-start.12 = (bf16[64,640]{1,0:T(8,128)(2,1)}, bf16[64,640]{1,0:T(8,128)(2,1)S(1)}, u32[]{:S(2)}) copy-start(bf16[64,640]{1,0:T(8,128)(2,1)S(1)} %collective-permute-done.19.refs_6_) | copy-start | bytes 245764
  114.0 9.8 %collective-permute-start.36 = (f32[16,1024]{1,0:T(8,128)S(1)}, f32[16,1024]{1,0:T(8,128)S(1)}, u32[]{:S(2)}, u32[]{:S(2)}) collective-permute-start(f32[16,1024]{1,0:T(8,128)S(1)} %add.38), channel_id=1, source_target_pairs={{0,64},{32,96},{64,0},{96,32},{128,192},{160,224},{192,128},{224,1... | collective-permute-start | bytes 196616 | tf_op jit(solution)/shard_map/ppermute | solution.py:320
  121.1 0.6 copy-start.13
  123.9 8.3 %collective-permute-start.37 = (f32[16,1024]{1,0:T(8,128)S(1)}, f32[16,1024]{1,0:T(8,128)S(1)}, u32[]{:S(2)}, u32[]{:S(2)}) collective-permute-start(f32[16,1024]{1,0:T(8,128)S(1)} %add.39), channel_id=1, source_target_pairs={{0,128},{32,160},{64,192},{96,224},{128,0},{160,32},{192,64},{224,... | collective-permute-start | bytes 196616 | tf_op jit(solution)/shard_map/ppermute | solution.py:320
  128.7 6.9 %collective-permute-start.26 = (bf16[128,256]{1,0:T(8,128)(2,1)S(1)}, bf16[128,256]{1,0:T(8,128)(2,1)S(1)}, u32[]{:S(2)}, u32[]{:S(2)}) collective-permute-start(bf16[128,256]{1,0:T(8,128)(2,1)S(1)} %get-tuple-element.65), channel_id=1, source_target_pairs={{0,8},{8,16},{16,24},{24,0},{1,9},{9,17},{17,25},{25,1},{2,10},{10... | collective-permute-start | bytes 196616 | tf_op jit(solution)/shard_map/ppermute | solution.py:245
  129.5 6.1 %collective-permute-start.25 = (bf16[128,256]{1,0:T(8,128)(2,1)S(1)}, bf16[128,256]{1,0:T(8,128)(2,1)S(1)}, u32[]{:S(2)}, u32[]{:S(2)}) collective-permute-start(bf16[128,256]{1,0:T(8,128)(2,1)S(1)} %get-tuple-element.66), channel_id=1, source_target_pairs={{0,16},{8,24},{16,0},{24,8},{1,17},{9,25},{17,1},{25,9},{2,18},{10... | collective-permute-start | bytes 196616 | tf_op jit(solution)/shard_map/ppermute | solution.py:245
  130.9 5.3 %collective-permute-start.24 = (bf16[128,256]{1,0:T(8,128)(2,1)S(1)}, bf16[128,256]{1,0:T(8,128)(2,1)S(1)}, u32[]{:S(2)}, u32[]{:S(2)}) collective-permute-start(bf16[128,256]{1,0:T(8,128)(2,1)S(1)} %get-tuple-element.67), channel_id=1, source_target_pairs={{0,24},{8,0},{16,8},{24,16},{1,25},{9,1},{17,9},{25,17},{2,26},{10... | collective-permute-start | bytes 196616 | tf_op jit(solution)/shard_map/ppermute | solution.py:245
  135.6 0.6 copy-start.3
  135.6 0.6 copy-start.4
  136.2 0.6 copy-start.5
  136.8 1.3 collective-permute-start.27
  138.2 0.6 copy-start.6

commit v2 on v1

--- a/solution.py
+++ b/solution.py
@@ -26,21 +26,22 @@
 TN = (((0,), (0,)), ((), ()))
 
 
-def call(body, out_shape, count, scratch=(), limit=None, name=None):
+def call(body, out_shape, count, scratch=(), limit=None, name=None, scalars=0, flops=1000):
     vm = pl.BlockSpec(memory_space=pltpu.VMEM)
     return pl.pallas_call(
         body,
         out_shape=out_shape,
-        in_specs=[pl.BlockSpec(memory_space=pltpu.SMEM)] + [vm] * count,
+        in_specs=[pl.BlockSpec(memory_space=pltpu.SMEM)] * scalars + [vm] * count,
         out_specs=jax.tree.map(lambda _: vm, out_shape),
         scratch_shapes=scratch,
+        cost_estimate=pl.CostEstimate(flops=flops, bytes_accessed=2 * 10**6, transcendentals=0),
         compiler_params=pltpu.CompilerParams(vmem_limit_bytes=limit),
         name=name,
     )
 
 
-def pack_keys_kernel(where, k_ref, v_ref, pk_ref, pv_ref, own_ref, swap_ref):
-    x, core = where[0], where[2]
+def pack_keys_kernel(k_ref, v_ref, pk_ref, pv_ref, own_ref, swap_ref):
+    x, core = lax.axis_index("x"), lax.axis_index("core")
     for s in range(4):
         head = lax.rem(x + s, 4)
         cols = pl.ds(pl.multiple_of(head * HD, HD), HD)
@@ -51,26 +52,26 @@
             out[s, OWN:, HD:] = pv_ref[:, cols]
 
 
-def pack_rows_kernel(where, q_ref, c_ref, t_ref, *outs):
-    x, core = where[0], where[2]
+def pack_rows_kernel(q_ref, c_ref, t_ref, own_ref, swap_ref):
+    x, core = lax.axis_index("x"), lax.axis_index("core")
     for s in range(4):
         head = lax.rem(x + s, 4)
         cols = pl.ds(pl.multiple_of(head * WIDE, HD), WIDE)
-        for out, member in ((outs[s], core), (outs[4 + s], 1 - core)):
-            out[:, 0:WIDE] = q_ref[member, :, cols]
-            out[:, WIDE : 2 * WIDE] = c_ref[member, :, cols]
+        for out, member in ((own_ref, core), (swap_ref, 1 - core)):
+            out[s, :, 0:WIDE] = q_ref[member, :, cols]
+            out[s, :, WIDE : 2 * WIDE] = c_ref[member, :, cols]
             left = t_ref[member, head]
             for part in range(3):
                 piece = left.astype(BF)
-                out[:, 2 * WIDE + part * GROUP : 2 * WIDE + (part + 1) * GROUP] = piece
+                out[s, :, 2 * WIDE + part * GROUP : 2 * WIDE + (part + 1) * GROUP] = piece
                 left = left - piece.astype(F32)
-            out[:, 2 * WIDE + 3 * GROUP :] = jnp.zeros((OWN, HD - 3 * GROUP), BF)
+            out[s, :, 2 * WIDE + 3 * GROUP :] = jnp.zeros((OWN, HD - 3 * GROUP), BF)
 
 
 def attend_kernel(step, where, *refs):
-    own, par, kvs = refs[0:4], refs[4:8], refs[8:12]
-    keep, other, grads, prompt_grads = refs[12:16], refs[16:20], refs[20:24], refs[24:28]
-    k_all, v_all, qc_all, t_all, q_st, c_st, prob, grad, dk, dv, dq_t, dq_all = refs[28:]
+    kvs, rows = refs[0:4], refs[4:8]
+    grads, prompt_grads, dqs = refs[8:12], refs[12:16], refs[16:20]
+    k_all, v_all, qc_all, t_all, q_st, c_st, prob, grad, dk, dv, dq_t, dq_all = refs[20:]
     x, z, core, length = where[0], where[1], where[2], where[3]
     sides = (core, 1 - core)
 
@@ -92,13 +93,15 @@
             v_all[slot : slot + 16] = kvs[j][row + OWN : row + 80, HD:]
     for s in range(4):
         xs = lax.rem(x + 4 - s, 4)
-        for side, ref in ((0, own[s]), (1, par[s])):
-            qc_all[xs, pl.ds(pl.multiple_of(OWN * sides[side], OWN), OWN)] = ref[...]
+        for side in range(2):
+            part = rows[s][side * OWN : (side + 1) * OWN]
+            qc_all[xs, pl.ds(pl.multiple_of(OWN * sides[side], OWN), OWN)] = part
     dk[...] = jnp.zeros_like(dk)
     dv[...] = jnp.zeros_like(dv)
     lane = lax.broadcasted_iota(jnp.int32, (1, SPAN), 1)
-    sub = lax.broadcasted_iota(jnp.int32, (SPAN, SPAN), 0)
-    col = lax.broadcasted_iota(jnp.int32, (SPAN, SPAN), 1)
+    sub = lax.broadcasted_iota(jnp.int32, (512, SPAN), 0)
+    col = lax.broadcasted_iota(jnp.int32, (512, SPAN), 1)
+    barred = jnp.where(sub <= col + z * SPAN, 0.0, 1e30)
 
     def block(b, carry):
         start = b * 512 + z * SPAN
@@ -149,14 +152,13 @@
             base = PROMPT + b * 512
 
             def tail(i, totals):
-                barred = jnp.where(sub + i * SPAN <= col + z * SPAN, 0.0, 1e30)
                 bar = thr + jnp.concatenate([barred] * GROUP, 1)
-                return first(pl.multiple_of(base + i * SPAN, SPAN), SPAN, bar, totals)
+                return first(pl.multiple_of(base, 512), 512, bar, totals)
 
             zero = jnp.zeros((8, ROWS), F32)
             steps = (1 + b) * (512 // step)
             totals = lax.fori_loop(0, steps, main, (zero, zero))
-            num, tot = lax.fori_loop(0, z + 1, tail, totals)
+            num, tot = tail(0, totals)
             mean = jnp.sum(tot, 0, keepdims=True) / jnp.maximum(
                 jnp.sum(num, 0, keepdims=True), 1.0
             )
@@ -181,7 +183,7 @@
                 return carry
 
             lax.fori_loop(0, steps, main2, 0)
-            lax.fori_loop(0, z + 1, tail2, 0)
+            second(pl.multiple_of(base, 512), 512)
             for h in range(GROUP):
                 dq_all[b, :, h * HD : (h + 1) * HD] = (
                     dq_t[:, h * SPAN : (h + 1) * SPAN].T * (1.0 / ROOT)
@@ -192,8 +194,9 @@
     lax.fori_loop(0, 4, block, 0)
     for s in range(4):
         to = lax.rem(x + s, 4)
-        for side, ref in ((0, keep[s]), (1, other[s])):
-            ref[...] = dq_all[to, pl.ds(pl.multiple_of(OWN * sides[side], OWN), OWN)]
+        for side in range(2):
+            part = dq_all[to, pl.ds(pl.multiple_of(OWN * sides[side], OWN), OWN)]
+            dqs[s][side * OWN : (side + 1) * OWN] = part
     for j in range(4):
         for part, total in ((0, dk), (1, dv)):
             cols = slice(part * HD, (part + 1) * HD)
@@ -203,18 +206,45 @@
                 grads[j][row : row + OWN, cols] = (total[pl.ds(at, OWN)] * (1.0 / ROOT)).astype(BF)
 
 
-def unpack_rows_kernel(where, *refs):
-    x, core = where[0], where[2]
-    out = refs[8]
+def attend(where, kvs, rows):
+    shape = jax.ShapeDtypeStruct
+    return call(
+        functools.partial(attend_kernel, 512),
+        [shape((512, 2 * HD), BF)] * 4 + [shape((128, 2 * HD), BF)] * 4 + [shape((SPAN, WIDE), BF)] * 4,
+        8,
+        [
+            pltpu.VMEM((KEYS, HD), BF),
+            pltpu.VMEM((KEYS, HD), BF),
+            pltpu.VMEM((4, SPAN, PACKED), BF),
+            pltpu.VMEM((GROUP, SPAN), F32),
+            pltpu.VMEM((ROWS, HD), BF),
+            pltpu.VMEM((ROWS, HD), BF),
+            pltpu.VMEM((KEYS, ROWS), BF),
+            pltpu.VMEM((KEYS, ROWS), F32),
+            pltpu.VMEM((KEYS, HD), F32),
+            pltpu.VMEM((KEYS, HD), F32),
+            pltpu.VMEM((HD, ROWS), F32),
+            pltpu.VMEM((4, SPAN, WIDE), BF),
+        ],
+        48 * 1024 * 1024,
+        "attend",
+        1,
+        6 * 10**9,
+    )(where, *kvs, *rows)
+
+
+def unpack_rows_kernel(*refs):
+    x, core = lax.axis_index("x"), lax.axis_index("core")
+    mine, swapped, out = refs[0:4], refs[4], refs[5]
     for s in range(4):
         head = lax.rem(x + 4 - s, 4)
         cols = pl.ds(pl.multiple_of(head * WIDE, HD), WIDE)
-        out[core, :, cols] = refs[s][...]
-        out[1 - core, :, cols] = refs[4 + s][...]
-
-
-def unpack_keys_kernel(where, *refs):
-    x, core = where[0], where[2]
+        out[core, :, cols] = mine[s][0:OWN]
+        out[1 - core, :, cols] = swapped[s]
+
+
+def unpack_keys_kernel(*refs):
+    x, core = lax.axis_index("x"), lax.axis_index("core")
     mine, swapped = refs[0:4], refs[4]
     out_k, out_v = refs[5:]
     for s in range(4):
@@ -226,8 +256,8 @@
         out_v[1 - core, :, cols] = swapped[s, :, HD:]
 
 
-def unpack_prompt_kernel(where, *refs):
-    x = where[0]
+def unpack_prompt_kernel(*refs):
+    x = lax.axis_index("x")
     mine, swapped = refs[0:4], refs[4]
     out = refs[5]
     for s in range(4):
@@ -247,11 +277,6 @@
 
 def swap(values):
     return lax.ppermute(values, "core", [(0, 1), (1, 0)])
-
-
-def shift_swap(values, by):
-    pairs = [(2 * i + c, 2 * ((i + by) % 4) + 1 - c) for i in range(4) for c in range(2)]
-    return lax.ppermute(values, ("x", "core"), pairs)
 
 
 def local(
@@ -270,52 +295,35 @@
     shape = jax.ShapeDtypeStruct
     kv_own, kv_swap = call(
         pack_keys_kernel, [shape((4, 80, 2 * HD), BF)] * 2, 4, name="pack_keys"
-    )(where, resp_keys, resp_values, prompt_key_matrix, prompt_value_matrix)
+    )(resp_keys, resp_values, prompt_key_matrix, prompt_value_matrix)
     kv_other = swap(kv_swap)
     chip = jnp.concatenate([kv_own, kv_other], 1)
     payload = jnp.concatenate([shift(chip[s], "x", s) for s in range(4)], 0)
+    thresh = jnp.transpose(thresholds.reshape(2, OWN, 4, GROUP), (0, 2, 1, 3))
+    rows_own, rows_swap = call(
+        pack_rows_kernel, [shape((4, OWN, PACKED), BF)] * 2, 3, name="pack_rows"
+    )(response_queries, response_cotangent, thresh)
+    rows_other = swap(rows_swap)
+    rows = [jnp.concatenate([rows_own[s], rows_other[s]], 0) for s in range(4)]
+    rows, payload = lax.optimization_barrier((rows, payload))
     kvs = [shift(payload, "z", j) for j in range(4)]
-
-    thresh = jnp.transpose(thresholds.reshape(2, OWN, 4, GROUP), (0, 2, 1, 3))
-    rows = call(pack_rows_kernel, [shape((OWN, PACKED), BF)] * 8, 3, name="pack_rows")(
-        where, response_queries, response_cotangent, thresh
-    )
-    own = [shift(rows[s], "x", s) for s in range(4)]
-    par = [shift_swap(rows[4 + s], s) for s in range(4)]
-
-    outs = call(
-        functools.partial(attend_kernel, 512),
-        [shape((OWN, WIDE), BF)] * 8 + [shape((512, 2 * HD), BF)] * 4 + [shape((128, 2 * HD), BF)] * 4,
-        12,
-        [
-            pltpu.VMEM((KEYS, HD), BF),
-            pltpu.VMEM((KEYS, HD), BF),
-            pltpu.VMEM((4, SPAN, PACKED), BF),
-            pltpu.VMEM((GROUP, SPAN), F32),
-            pltpu.VMEM((ROWS, HD), BF),
-            pltpu.VMEM((ROWS, HD), BF),
-            pltpu.VMEM((KEYS, ROWS), BF),
-            pltpu.VMEM((KEYS, ROWS), F32),
-            pltpu.VMEM((KEYS, HD), F32),
-            pltpu.VMEM((KEYS, HD), F32),
-            pltpu.VMEM((HD, ROWS), F32),
-            pltpu.VMEM((4, SPAN, WIDE), BF),
-        ],
-        48 * 1024 * 1024,
-        "attend",
-    )(where, *own, *par, *kvs)
-    keep, other, grads, prompt_grads = outs[0:4], outs[4:8], outs[8:12], outs[12:16]
+    rows = [shift(rows[s], "x", s) for s in range(4)]
+    outs = attend(where, kvs, rows)
+    grads, prompt_grads, dqs = outs[0:4], outs[4:8], outs[8:12]
 
     def summed(parts):
         got = [shift(parts[j], "z", -j).astype(F32) for j in range(4)]
         return (got[0] + got[1] + got[2] + got[3]).astype(BF)
 
     prompt_sum = summed(prompt_grads)
+    dqs, prompt_sum = lax.optimization_barrier((dqs, prompt_sum))
     prompt_back = [shift(prompt_sum[32 * s : 32 * s + 32], "x", -s) for s in range(4)]
     prompt_swapped = swap(jnp.stack([p[OWN_PROMPT:] for p in prompt_back]))
     prompt_total = call(unpack_prompt_kernel, shape((OWN_PROMPT, 8 * HD), F32), 5, name="unpack_prompt")(
-        where, *prompt_back, prompt_swapped
+        *prompt_back, prompt_swapped
     )
+    key_sum = summed(grads)
+    key_sum, prompt_total = lax.optimization_barrier((key_sum, prompt_total))
     for mask in (1, 2, 4):
         prompt_total = prompt_total + lax.ppermute(
             prompt_total, "resp", [(i, i ^ mask) for i in range(8)]
@@ -323,18 +331,17 @@
     grad_prompt_keys = prompt_total[:, : 4 * HD].astype(BF)
     grad_prompt_values = prompt_total[:, 4 * HD :].astype(BF)
 
-    back_own = [shift(keep[s], "x", s) for s in range(4)]
-    back_par = [shift_swap(other[s], s) for s in range(4)]
-    grad_queries = call(unpack_rows_kernel, shape((2, OWN, 4 * WIDE), BF), 8, name="unpack_rows")(
-        where, *back_own, *back_par
+    row_back = [shift(dqs[s], "x", s) for s in range(4)]
+    row_swapped = swap(jnp.stack([r[OWN:] for r in row_back]))
+    grad_queries = call(unpack_rows_kernel, shape((2, OWN, 4 * WIDE), BF), 5, name="unpack_rows")(
+        *row_back, row_swapped
     )
 
-    key_sum = summed(grads)
     key_back = [shift(key_sum[SPAN * s : SPAN * (s + 1)], "x", -s) for s in range(4)]
     key_swapped = swap(jnp.stack([p[OWN:] for p in key_back]))
     grad_resp_keys, grad_resp_values = call(
         unpack_keys_kernel, [shape((2, OWN, 4 * HD), BF)] * 2, 5, name="unpack_keys"
-    )(where, *key_back, key_swapped)
+    )(*key_back, key_swapped)
     return (grad_queries, grad_resp_keys, grad_resp_values, grad_prompt_keys, grad_prompt_values)
 
 

time: 143 us -> 132 us (0.923)
  the two profiles are of different devices: /device:TPU:24 before, /device:TPU:70 now
where the time goes in v2:
time: 132 us; the launch traced here: 131 us
  waiting for transfers between devices  46.7 us (35%)
  starting transfers between devices  44 us (33%)
  Pallas kernels  29 us (22%)
  local copies, waits for them, and re-layouts  7.83 us (6%)
  other arithmetic  2.6 us (2%)
    ppermute x24, waiting for transfers between devices, shift(): return lax.ppermute(values, axis, [(i, (i + by) % 4) for i in range(4)])  34.4 us
    ppermute x24, starting transfers between devices, shift(): return lax.ppermute(values, axis, [(i, (i + by) % 4) for i in range(4)])  31.7 us
    pallas_call x1, Pallas kernels, attend(): call(functools.partial(attend_kernel, 512), [shape((512, 2 * HD), BF)] *...  19.1 us
    ppermute x3, starting transfers between devices, local(): lax.ppermute(prompt_total, 'resp', [(i, i ^ mask) for i in range(8)])  11.7 us
    ppermute x3, waiting for transfers between devices, local(): lax.ppermute(prompt_total, 'resp', [(i, i ^ mask) for i in range(8)])  11.1 us
    unnamed x41, local copies, waits for them, and re-layouts  4.33 us
    pallas_call x1, Pallas kernels, local(): call(pack_rows_kernel, [shape((4, OWN, PACKED), BF)] * 2, 3, name='pack_r...  2.74 us
  transfers between devices with their start and end apart: 32, of which 14 were waited for; matrix products, arithmetic and copies ran while one was open for 3% of the time, Pallas kernels for 5%

profile of v2, /device:TPU:70, one launch (start us, length us, event | category | flops | bytes accessed | tf_op | source)
XLA Modules:
  0.0 131.1 jit_solution(5010431770332995366)
XLA Ops:
  0.6 1.8 %pack_keys.1 = (bf16[4,80,256]{2,1,0:T(8,128)(2,1)}, bf16[4,80,256]{2,1,0:T(8,128)(2,1)}) custom-call(bf16[2,64,512]{2,1,0:T(8,128)(2,1)} %k_ref.1, bf16[2,64,512]{2,1,0:T(8,128)(2,1)} %v_ref.1, bf16[16,512]{1,0:T(8,128)(2,1)} %pk_ref.1, bf16[16,512]{1,0:T(8,128)(2,1)} %pv_ref.1), custom_call_target="tpu_custom_call" | custom-call | flops 1000 | bytes 2000000 | tf_op jit(solution)/shard_map/pack_keys/pallas_call | solution.py:296
  2.4 0.9 copy.13
  3.3 2.7 %pack_rows.1 = (bf16[4,64,1408]{2,1,0:T(8,128)(2,1)}, bf16[4,64,1408]{2,1,0:T(8,128)(2,1)}) custom-call(bf16[2,64,2560]{2,1,0:T(8,128)(2,1)} %q_ref.1, bf16[2,64,2560]{2,1,0:T(8,128)(2,1)} %c_ref.1, f32[2,4,64,5]{3,2,1,0:T(8,128)} %bitcast.53), custom_call_target="tpu_custom_call" | custom-call | flops 1000 | bytes 2000000 | tf_op jit(solution)/shard_map/pack_rows/pallas_call | solution.py:303
  6.0 0.5 collective-permute-start
  6.6 0.9 collective-permute-start.4
  7.5 1.1 collective-permute-start.3
  8.6 2.1 %collective-permute-start.2 = (bf16[160,256]{1,0:T(8,128)(2,1)S(1)}, bf16[160,256]{1,0:T(8,128)(2,1)S(1)}, u32[]{:S(2)}, u32[]{:S(2)}) collective-permute-start(bf16[160,256]{1,0:T(8,128)(2,1)S(1)} %get-tuple-element.76), channel_id=1, source_target_pairs={{0,8},{8,16},{16,24},{24,0},{1,9},{9,17},{17,25},{25,1},{2,10},{10... | collective-permute-start | bytes 245768 | tf_op jit(solution)/shard_map/ppermute | solution.py:275
  10.7 0.1 slice_bitcast_fusion.4
  10.8 3.2 %collective-permute-done.4 = bf16[160,256]{1,0:T(8,128)(2,1)S(1)} collective-permute-done((bf16[160,256]{1,0:T(8,128)(2,1)S(1)}, bf16[160,256]{1,0:T(8,128)(2,1)S(1)}, u32[]{:S(2)}, u32[]{:S(2)}) %collective-permute-start.4) | collective-permute-done | bytes 81952 | tf_op jit(solution)/shard_map/ppermute | solution.py:275
  14.0 0.6 collective-permute-done.2
  14.6 0.1 slice_bitcast_fusion
  14.7 0.8 pad_maximum_fusion.2
  15.5 0.8 pad_maximum_fusion
  16.3 0.1 collective-permute-start.7
  16.4 2.7 %collective-permute-start.8 = (bf16[128,1408]{1,0:T(8,128)(2,1)}, bf16[128,1408]{1,0:T(8,128)(2,1)S(1)}, u32[]{:S(2)}, u32[]{:S(2)}) collective-permute-start(bf16[128,1408]{1,0:T(8,128)(2,1)} %get-tuple-element.41), channel_id=1, source_target_pairs={{0,8},{8,16},{16,24},{24,0},{1,9},{9,17},{17,25},{25,1},{2,10},{10... | collective-permute-start | bytes 1081352 | tf_op jit(solution)/shard_map/ppermute | solution.py:275
  19.1 0.3 collective-permute-start.9
  19.3 0.6 collective-permute-start.10
  19.9 4.2 %collective-permute-start.6 = (bf16[640,256]{1,0:T(8,128)(2,1)S(1)}, bf16[640,256]{1,0:T(8,128)(2,1)S(1)}, u32[]{:S(2)}, u32[]{:S(2)}) collective-permute-start(bf16[640,256]{1,0:T(8,128)(2,1)S(1)} %pad_maximum_fusion.4.refs_0_), channel_id=1, source_target_pairs={{0,4},{2,6},{4,0},{6,2},{1,5},{3,7},{5,1},{7,3},{8,12},{10,14},{12... | collective-permute-start | bytes 983048 | tf_op jit(solution)/shard_map/ppermute | solution.py:275
  24.1 2.8 %collective-permute-done.7.refs_3_ = bf16[640,256]{1,0:T(8,128)(2,1)S(1)} collective-permute-done((bf16[640,256]{1,0:T(8,128)(2,1)S(1)}, bf16[640,256]{1,0:T(8,128)(2,1)S(1)}, u32[]{:S(2)}, u32[]{:S(2)}) %collective-permute-start.7) | collective-permute-done | bytes 327712 | tf_op jit(solution)/shard_map/ppermute | solution.py:275
  26.9 3.8 %collective-permute-start.5 = (bf16[640,256]{1,0:T(8,128)(2,1)S(1)}, bf16[640,256]{1,0:T(8,128)(2,1)S(1)}, u32[]{:S(2)}, u32[]{:S(2)}) collective-permute-start(bf16[640,256]{1,0:T(8,128)(2,1)S(1)} %pad_maximum_fusion.4.refs_0_), channel_id=1, source_target_pairs={{0,2},{2,4},{4,6},{6,0},{1,3},{3,5},{5,7},{7,1},{8,10},{10,12},{12... | collective-permute-start | bytes 983048 | tf_op jit(solution)/shard_map/ppermute | solution.py:275
  30.7 0.7 copy-done.19
  31.4 0.6 dynamic_slice.4
  32.0 0.7 pad_add_fusion.where
  32.7 10.9 %collective-permute-done.6.refs_2_ = bf16[640,256]{1,0:T(8,128)(2,1)S(1)} collective-permute-done((bf16[640,256]{1,0:T(8,128)(2,1)S(1)}, bf16[640,256]{1,0:T(8,128)(2,1)S(1)}, u32[]{:S(2)}, u32[]{:S(2)}) %collective-permute-start.6) | collective-permute-done | bytes 327712 | tf_op jit(solution)/shard_map/ppermute | solution.py:275
  43.6 4.5 %collective-permute-done.5.refs_1_ = bf16[640,256]{1,0:T(8,128)(2,1)S(1)} collective-permute-done((bf16[640,256]{1,0:T(8,128)(2,1)S(1)}, bf16[640,256]{1,0:T(8,128)(2,1)S(1)}, u32[]{:S(2)}, u32[]{:S(2)}) %collective-permute-start.5) | collective-permute-done | bytes 327712 | tf_op jit(solution)/shard_map/ppermute | solution.py:275
  48.1 19.1 %attend.1 = (bf16[512,256]{1,0:T(8,128)(2,1)S(1)}, bf16[512,256]{1,0:T(8,128)(2,1)}, bf16[512,256]{1,0:T(8,128)(2,1)}, bf16[512,256]{1,0:T(8,128)(2,1)S(1)}, bf1...) custom-call(s32[4]{0:T(128)S(1)} %pad_add_fusion.where, ...), custom_call_target="tpu_custom_call" | custom-call | flops 6000000000 | bytes 2000000 | tf_op jit(solution)/shard_map/attend/pallas_call | solution.py:211
  67.2 0.2 collective-permute-start.11
  67.4 0.1 collective-permute-start.12
  67.5 1.9 %collective-permute-start.13 = (bf16[128,256]{1,0:T(8,128)(2,1)S(1)}, bf16[128,256]{1,0:T(8,128)(2,1)S(1)}, u32[]{:S(2)}, u32[]{:S(2)}) collective-permute-start(bf16[128,256]{1,0:T(8,128)(2,1)S(1)} %get-tuple-element.51), channel_id=1, source_target_pairs={{0,2},{2,4},{4,6},{6,0},{1,3},{3,5},{5,7},{7,1},{8,10},{10,12},{12... | collective-permute-start | bytes 196616 | tf_op jit(solution)/shard_map/ppermute | solution.py:275
  69.4 1.5 %collective-permute-start.18 = (bf16[512,256]{1,0:T(8,128)(2,1)}, bf16[512,256]{1,0:T(8,128)(2,1)S(1)}, u32[]{:S(2)}, u32[]{:S(2)}) collective-permute-start(bf16[512,256]{1,0:T(8,128)(2,1)} %get-tuple-element.57), channel_id=1, source_target_pairs={{0,6},{2,0},{4,2},{6,4},{1,7},{3,1},{5,3},{7,5},{8,14},{10,8},{12,... | collective-permute-start | bytes 786440 | tf_op jit(solution)/shard_map/ppermute | solution.py:275
  70.9 3.4 %collective-permute-start.19 = (bf16[512,256]{1,0:T(8,128)(2,1)}, bf16[512,256]{1,0:T(8,128)(2,1)S(1)}, u32[]{:S(2)}, u32[]{:S(2)}) collective-permute-start(bf16[512,256]{1,0:T(8,128)(2,1)} %get-tuple-element.58), channel_id=1, source_target_pairs={{0,4},{2,6},{4,0},{6,2},{1,5},{3,7},{5,1},{7,3},{8,12},{10,14},{12... | collective-permute-start | bytes 786440 | tf_op jit(solution)/shard_map/ppermute | solution.py:275
  74.2 0.1 collective-permute-start.20
  74.4 1.4 %collective-permute-done.13 = bf16[128,256]{1,0:T(8,128)(2,1)S(1)} collective-permute-done((bf16[128,256]{1,0:T(8,128)(2,1)S(1)}, bf16[128,256]{1,0:T(8,128)(2,1)S(1)}, u32[]{:S(2)}, u32[]{:S(2)}) %collective-permute-start.13) | collective-permute-done | bytes 65568 | tf_op jit(solution)/shard_map/ppermute | solution.py:275
  75.8 0.6 fusion.1
  76.4 3.2 %collective-permute-start.23 = (bf16[32,256]{1,0:T(8,128)(2,1)S(1)}, bf16[32,256]{1,0:T(8,128)(2,1)S(1)}, u32[]{:S(2)}, u32[]{:S(2)}) collective-permute-start(bf16[32,256]{1,0:T(8,128)(2,1)S(1)} %get-tuple-element.81), channel_id=1, source_target_pairs={{0,8},{8,16},{16,24},{24,0},{1,9},{9,17},{17,25},{25,1},{2,10},{10... | collective-permute-start | bytes 49160 | tf_op jit(solution)/shard_map/ppermute | solution.py:275
  79.7 1.4 %collective-permute-done.23.refs_3_ = bf16[32,256]{1,0:T(8,128)(2,1)S(1)} collective-permute-done((bf16[32,256]{1,0:T(8,128)(2,1)S(1)}, bf16[32,256]{1,0:T(8,128)(2,1)S(1)}, u32[]{:S(2)}, u32[]{:S(2)}) %collective-permute-start.23) | collective-permute-done | bytes 16416 | tf_op jit(solution)/shard_map/ppermute | solution.py:275
  81.1 3.8 %collective-permute-done.22.refs_2_ = bf16[32,256]{1,0:T(8,128)(2,1)S(1)} collective-permute-done((bf16[32,256]{1,0:T(8,128)(2,1)S(1)}, bf16[32,256]{1,0:T(8,128)(2,1)S(1)}, u32[]{:S(2)}, u32[]{:S(2)}) %collective-permute-start.22) | collective-permute-done | bytes 16416 | tf_op jit(solution)/shard_map/ppermute | solution.py:275
  84.9 1.4 %collective-permute-done.21.refs_1_ = bf16[32,256]{1,0:T(8,128)(2,1)S(1)} collective-permute-done((bf16[32,256]{1,0:T(8,128)(2,1)S(1)}, bf16[32,256]{1,0:T(8,128)(2,1)S(1)}, u32[]{:S(2)}, u32[]{:S(2)}) %collective-permute-start.21) | collective-permute-done | bytes 16416 | tf_op jit(solution)/shard_map/ppermute | solution.py:275
  86.4 0.6 copy-done.16
  87.0 1.2 collective-permute-done.24.refs_4_
  88.2 1.2 collective-permute-start.15
  89.4 1.5 %unpack_prompt.1 = f32[16,1024]{1,0:T(8,128)} custom-call(bf16[32,256]{1,0:T(8,128)(2,1)} %get-tuple-element.84.refs_0_, bf16[32,256]{1,0:T(8,128)(2,1)} %copy-done.16, bf16[32,256]{1,0:T(8,128)(2,1)} %copy-done.15, bf16[32,256]{1,0:T(8,128)(2,1)} %copy-done.14, bf16[4,16,256]{2,1,0:T(8,128)(2,1)} %copy-done.17), custom_call_target="tpu_custom_call" | custom-call | flops 1000 | bytes 2000000 | tf_op jit(solution)/shard_map/unpack_prompt/pallas_call | solution.py:322
  90.8 1.8 %collective-permute-start.16 = (bf16[128,640]{1,0:T(8,128)(2,1)S(1)}, bf16[128,640]{1,0:T(8,128)(2,1)S(1)}, u32[]{:S(2)}, u32[]{:S(2)}) collective-permute-start(bf16[128,640]{1,0:T(8,128)(2,1)S(1)} %copy-done.2), channel_id=1, source_target_pairs={{0,24},{8,0},{16,8},{24,16},{1,25},{9,1},{17,9},{25,17},{2,26},{10... | collective-permute-start | bytes 491528 | tf_op jit(solution)/shard_map/ppermute | solution.py:275
  92.6 4.3 %collective-permute-done.15.refs_2_ = bf16[128,640]{1,0:T(8,128)(2,1)S(1)} collective-permute-done((bf16[128,640]{1,0:T(8,128)(2,1)}, bf16[128,640]{1,0:T(8,128)(2,1)S(1)}, u32[]{:S(2)}, u32[]{:S(2)}) %collective-permute-start.15) | collective-permute-done | bytes 163872 | tf_op jit(solution)/shard_map/ppermute | solution.py:275
  97.0 0.1 add_convert_fusion
  97.1 0.5 copy-done.5
  97.6 0.6 fusion
  98.2 1.2 collective-permute-start.27
  99.5 0.7 collective-permute-start.26
  100.2 0.6 collective-permute-start.25
  100.8 7.0 %collective-permute-done.29 = f32[16,1024]{1,0:T(8,128)S(1)} collective-permute-done((f32[16,1024]{1,0:T(8,128)S(1)}, f32[16,1024]{1,0:T(8,128)S(1)}, u32[]{:S(2)}, u32[]{:S(2)}) %collective-permute-start.29) | collective-permute-done | bytes 65568 | tf_op jit(solution)/shard_map/ppermute | solution.py:328
  107.8 11.6 %collective-permute-start.30 = (f32[16,1024]{1,0:T(8,128)S(1)}, f32[16,1024]{1,0:T(8,128)S(1)}, u32[]{:S(2)}, u32[]{:S(2)}) collective-permute-start(f32[16,1024]{1,0:T(8,128)S(1)} %add.38), channel_id=1, source_target_pairs={{0,64},{32,96},{64,0},{96,32},{128,192},{160,224},{192,128},{224,1... | collective-permute-start | bytes 196616 | tf_op jit(solution)/shard_map/ppermute | solution.py:328
  119.4 0.6 copy-done.10
  120.1 0.6 copy-done.12
  120.7 1.0 collective-permute-done.30
  121.7 0.1 collective-permute-start.31
  121.8 0.1 pad_maximum_fusion.5
  121.8 0.1 collective-permute-start.17
  122.0 0.7 copy-done.13
  122.6 1.8 %unpack_keys.1 = (bf16[2,64,512]{2,1,0:T(8,128)(2,1)}, bf16[2,64,512]{2,1,0:T(8,128)(2,1)}) custom-call(bf16[128,256]{1,0:T(8,128)(2,1)} %get-tuple-element.80.refs_0_, bf16[128,256]{1,0:T(8,128)(2,1)} %copy-done.12, bf16[128,256]{1,0:T(8,128)(2,1)} %copy-done.11, bf16[128,256]{1,0:T(8,128)(2,1)} %copy-done.10, bf16[4,64,256]{2,1,0:T(8,128)(2,1)} %copy-done.13), custom_call_target="tpu_custom_call" | custom-call | flops 1000 | bytes 2000000 | tf_op jit(solution)/shard_map/unpack_keys/pallas_call | solution.py:342
  124.4 3.1 %collective-permute-done.31 = f32[16,1024]{1,0:T(8,128)S(1)} collective-permute-done((f32[16,1024]{1,0:T(8,128)S(1)}, f32[16,1024]{1,0:T(8,128)S(1)}, u32[]{:S(2)}, u32[]{:S(2)}) %collective-permute-start.31) | collective-permute-done | bytes 65568 | tf_op jit(solution)/shard_map/ppermute | solution.py:328
  127.5 0.6 fusion.2
  128.2 0.7 copy-done.7
  128.9 2.2 %unpack_rows.1 = bf16[2,64,2560]{2,1,0:T(8,128)(2,1)} custom-call(bf16[128,640]{1,0:T(8,128)(2,1)} %copy-done, bf16[128,640]{1,0:T(8,128)(2,1)} %copy-done.4, bf16[128,640]{1,0:T(8,128)(2,1)} %copy-done.5, bf16[128,640]{1,0:T(8,128)(2,1)} %copy-done.6, bf16[4,64,640]{2,1,0:T(8,128)(2,1)} %copy-done.7), custom_call_target="tpu_custom_call" | custom-call | flops 1000 | bytes 2000000 | tf_op jit(solution)/shard_map/unpack_rows/pallas_call | solution.py:336
  (80 shorter events, 0.4 us)
Async XLA Ops:
  0.6 1.8 %copy-start.18 = (f32[2,64,20]{1,0,2:T(2,128)S(1)}, f32[2,64,20]{1,0,2:T(2,128)}, u32[]{:S(2)}) copy-start(f32[2,64,20]{1,0,2:T(2,128)} %param.14) | copy-start | bytes 30724
  2.4 4.1 %collective-permute-start.1 = (bf16[4,80,256]{2,1,0:T(8,128)(2,1)}, bf16[4,80,256]{2,1,0:T(8,128)(2,1)S(1)}, u32[]{:S(2)}, u32[]{:S(2)}) collective-permute-start(bf16[4,80,256]{2,1,0:T(8,128)(2,1)} %get-tuple-element.38), channel_id=1, source_target_pairs={{0,1},{1,0},{2,3},{3,2},{4,5},{5,4},{6,7},{7,6},{8,9},{9,8},{10,11... | collective-permute-start | bytes 491528 | tf_op jit(solution)/shard_map/ppermute | solution.py:279
  3.3 3.3 %copy-start.9 = (bf16[4,80,256]{2,1,0:T(8,128)(2,1)S(1)}, bf16[4,80,256]{2,1,0:T(8,128)(2,1)}, u32[]{:S(2)}) copy-start(bf16[4,80,256]{2,1,0:T(8,128)(2,1)} %get-tuple-element.37) | copy-start | bytes 491524
  6.0 4.7 %copy-start.3 = (bf16[4,64,1408]{2,1,0:T(8,128)(2,1)S(1)}, bf16[4,64,1408]{2,1,0:T(8,128)(2,1)}, u32[]{:S(2)}) copy-start(bf16[4,64,1408]{2,1,0:T(8,128)(2,1)} %get-tuple-element.35) | copy-start | bytes 2162692
  6.0 8.6 %collective-permute-start = (bf16[4,64,1408]{2,1,0:T(8,128)(2,1)}, bf16[4,64,1408]{2,1,0:T(8,128)(2,1)S(1)}, u32[]{:S(2)}, u32[]{:S(2)}) collective-permute-start(bf16[4,64,1408]{2,1,0:T(8,128)(2,1)} %get-tuple-element.36), channel_id=1, source_target_pairs={{0,1},{1,0},{2,3},{3,2},{4,5},{5,4},{6,7},{7,6},{8,9},{9,8},{10,11... | collective-permute-start | bytes 2162696 | tf_op jit(solution)/shard_map/ppermute | solution.py:279
  6.6 7.4 %collective-permute-start.4 = (bf16[160,256]{1,0:T(8,128)(2,1)S(1)}, bf16[160,256]{1,0:T(8,128)(2,1)S(1)}, u32[]{:S(2)}, u32[]{:S(2)}) collective-permute-start(bf16[160,256]{1,0:T(8,128)(2,1)S(1)} %get-tuple-element.74), channel_id=1, source_target_pairs={{0,24},{8,0},{16,8},{24,16},{1,25},{9,1},{17,9},{25,17},{2,26},{10... | collective-permute-start | bytes 245768 | tf_op jit(solution)/shard_map/ppermute | solution.py:275
  7.5 6.5 %collective-permute-start.3 = (bf16[160,256]{1,0:T(8,128)(2,1)S(1)}, bf16[160,256]{1,0:T(8,128)(2,1)S(1)}, u32[]{:S(2)}, u32[]{:S(2)}) collective-permute-start(bf16[160,256]{1,0:T(8,128)(2,1)S(1)} %get-tuple-element.75), channel_id=1, source_target_pairs={{0,16},{8,24},{16,0},{24,8},{1,17},{9,25},{17,1},{25,9},{2,18},{10... | collective-permute-start | bytes 245768 | tf_op jit(solution)/shard_map/ppermute | solution.py:275
  8.6 6.0 %collective-permute-start.2 = (bf16[160,256]{1,0:T(8,128)(2,1)S(1)}, bf16[160,256]{1,0:T(8,128)(2,1)S(1)}, u32[]{:S(2)}, u32[]{:S(2)}) collective-permute-start(bf16[160,256]{1,0:T(8,128)(2,1)S(1)} %get-tuple-element.76), channel_id=1, source_target_pairs={{0,8},{8,16},{16,24},{24,0},{1,9},{9,17},{17,25},{25,1},{2,10},{10... | collective-permute-start | bytes 245768 | tf_op jit(solution)/shard_map/ppermute | solution.py:275
  16.3 10.7 %collective-permute-start.7 = (bf16[640,256]{1,0:T(8,128)(2,1)S(1)}, bf16[640,256]{1,0:T(8,128)(2,1)S(1)}, u32[]{:S(2)}, u32[]{:S(2)}) collective-permute-start(bf16[640,256]{1,0:T(8,128)(2,1)S(1)} %pad_maximum_fusion.4.refs_0_), channel_id=1, source_target_pairs={{0,6},{2,0},{4,2},{6,4},{1,7},{3,1},{5,3},{7,5},{8,14},{10,8},{12,... | collective-permute-start | bytes 983048 | tf_op jit(solution)/shard_map/ppermute | solution.py:275
  16.4 31.7 %collective-permute-start.8 = (bf16[128,1408]{1,0:T(8,128)(2,1)}, bf16[128,1408]{1,0:T(8,128)(2,1)S(1)}, u32[]{:S(2)}, u32[]{:S(2)}) collective-permute-start(bf16[128,1408]{1,0:T(8,128)(2,1)} %get-tuple-element.41), channel_id=1, source_target_pairs={{0,8},{8,16},{16,24},{24,0},{1,9},{9,17},{17,25},{25,1},{2,10},{10... | collective-permute-start | bytes 1081352 | tf_op jit(solution)/shard_map/ppermute | solution.py:275
  19.1 29.0 %collective-permute-start.9 = (bf16[128,1408]{1,0:T(8,128)(2,1)}, bf16[128,1408]{1,0:T(8,128)(2,1)S(1)}, u32[]{:S(2)}, u32[]{:S(2)}) collective-permute-start(bf16[128,1408]{1,0:T(8,128)(2,1)} %get-tuple-element.42), channel_id=1, source_target_pairs={{0,16},{8,24},{16,0},{24,8},{1,17},{9,25},{17,1},{25,9},{2,18},{10... | collective-permute-start | bytes 1081352 | tf_op jit(solution)/shard_map/ppermute | solution.py:275
  19.3 28.8 %collective-permute-start.10 = (bf16[128,1408]{1,0:T(8,128)(2,1)S(1)}, bf16[128,1408]{1,0:T(8,128)(2,1)S(1)}, u32[]{:S(2)}, u32[]{:S(2)}) collective-permute-start(bf16[128,1408]{1,0:T(8,128)(2,1)S(1)} %get-tuple-element.43), channel_id=1, source_target_pairs={{0,24},{8,0},{16,8},{24,16},{1,25},{9,1},{17,9},{25,17},{2,26},{10... | collective-permute-start | bytes 1081352 | tf_op jit(solution)/shard_map/ppermute | solution.py:275
  19.9 23.7 %collective-permute-start.6 = (bf16[640,256]{1,0:T(8,128)(2,1)S(1)}, bf16[640,256]{1,0:T(8,128)(2,1)S(1)}, u32[]{:S(2)}, u32[]{:S(2)}) collective-permute-start(bf16[640,256]{1,0:T(8,128)(2,1)S(1)} %pad_maximum_fusion.4.refs_0_), channel_id=1, source_target_pairs={{0,4},{2,6},{4,0},{6,2},{1,5},{3,7},{5,1},{7,3},{8,12},{10,14},{12... | collective-permute-start | bytes 983048 | tf_op jit(solution)/shard_map/ppermute | solution.py:275
  26.9 21.2 %collective-permute-start.5 = (bf16[640,256]{1,0:T(8,128)(2,1)S(1)}, bf16[640,256]{1,0:T(8,128)(2,1)S(1)}, u32[]{:S(2)}, u32[]{:S(2)}) collective-permute-start(bf16[640,256]{1,0:T(8,128)(2,1)S(1)} %pad_maximum_fusion.4.refs_0_), channel_id=1, source_target_pairs={{0,2},{2,4},{4,6},{6,0},{1,3},{3,5},{5,7},{7,1},{8,10},{10,12},{12... | collective-permute-start | bytes 983048 | tf_op jit(solution)/shard_map/ppermute | solution.py:275
  30.7 0.7 copy-start.19
  67.2 8.6 %copy-start.1 = (bf16[128,640]{1,0:T(8,128)(2,1)}, bf16[128,640]{1,0:T(8,128)(2,1)S(1)}, u32[]{:S(2)}) copy-start(bf16[128,640]{1,0:T(8,128)(2,1)S(1)} %get-tuple-element.55) | copy-start | bytes 491524
  67.2 19.8 %copy-start = (bf16[128,640]{1,0:T(8,128)(2,1)}, bf16[128,640]{1,0:T(8,128)(2,1)S(1)}, u32[]{:S(2)}) copy-start(bf16[128,640]{1,0:T(8,128)(2,1)S(1)} %get-tuple-element.52.refs_0_) | copy-start | bytes 491524
  67.2 7.0 %collective-permute-start.11 = (bf16[128,256]{1,0:T(8,128)(2,1)S(1)}, bf16[128,256]{1,0:T(8,128)(2,1)S(1)}, u32[]{:S(2)}, u32[]{:S(2)}) collective-permute-start(bf16[128,256]{1,0:T(8,128)(2,1)S(1)} %get-tuple-element.49), channel_id=1, source_target_pairs={{0,6},{2,0},{4,2},{6,4},{1,7},{3,1},{5,3},{7,5},{8,14},{10,8},{12,... | collective-permute-start | bytes 196616 | tf_op jit(solution)/shard_map/ppermute | solution.py:275
  67.4 7.0 %collective-permute-start.12 = (bf16[128,256]{1,0:T(8,128)(2,1)S(1)}, bf16[128,256]{1,0:T(8,128)(2,1)S(1)}, u32[]{:S(2)}, u32[]{:S(2)}) collective-permute-start(bf16[128,256]{1,0:T(8,128)(2,1)S(1)} %get-tuple-element.50), channel_id=1, source_target_pairs={{0,4},{2,6},{4,0},{6,2},{1,5},{3,7},{5,1},{7,3},{8,12},{10,14},{12... | collective-permute-start | bytes 196616 | tf_op jit(solution)/shard_map/ppermute | solution.py:275
  67.5 8.3 %collective-permute-start.13 = (bf16[128,256]{1,0:T(8,128)(2,1)S(1)}, bf16[128,256]{1,0:T(8,128)(2,1)S(1)}, u32[]{:S(2)}, u32[]{:S(2)}) collective-permute-start(bf16[128,256]{1,0:T(8,128)(2,1)S(1)} %get-tuple-element.51), channel_id=1, source_target_pairs={{0,2},{2,4},{4,6},{6,0},{1,3},{3,5},{5,7},{7,1},{8,10},{10,12},{12... | collective-permute-start | bytes 196616 | tf_op jit(solution)/shard_map/ppermute | solution.py:275
  69.4 27.5 %collective-permute-start.18 = (bf16[512,256]{1,0:T(8,128)(2,1)}, bf16[512,256]{1,0:T(8,128)(2,1)S(1)}, u32[]{:S(2)}, u32[]{:S(2)}) collective-permute-start(bf16[512,256]{1,0:T(8,128)(2,1)} %get-tuple-element.57), channel_id=1, source_target_pairs={{0,6},{2,0},{4,2},{6,4},{1,7},{3,1},{5,3},{7,5},{8,14},{10,8},{12,... | collective-permute-start | bytes 786440 | tf_op jit(solution)/shard_map/ppermute | solution.py:275
  70.9 26.1 %collective-permute-start.19 = (bf16[512,256]{1,0:T(8,128)(2,1)}, bf16[512,256]{1,0:T(8,128)(2,1)S(1)}, u32[]{:S(2)}, u32[]{:S(2)}) collective-permute-start(bf16[512,256]{1,0:T(8,128)(2,1)} %get-tuple-element.58), channel_id=1, source_target_pairs={{0,4},{2,6},{4,0},{6,2},{1,5},{3,7},{5,1},{7,3},{8,12},{10,14},{12... | collective-permute-start | bytes 786440 | tf_op jit(solution)/shard_map/ppermute | solution.py:275
  74.2 22.7 %collective-permute-start.20 = (bf16[512,256]{1,0:T(8,128)(2,1)S(1)}, bf16[512,256]{1,0:T(8,128)(2,1)S(1)}, u32[]{:S(2)}, u32[]{:S(2)}) collective-permute-start(bf16[512,256]{1,0:T(8,128)(2,1)S(1)} %get-tuple-element.59), channel_id=1, source_target_pairs={{0,2},{2,4},{4,6},{6,0},{1,3},{3,5},{5,7},{7,1},{8,10},{10,12},{12... | collective-permute-start | bytes 786440 | tf_op jit(solution)/shard_map/ppermute | solution.py:275
  76.4 4.7 %collective-permute-start.23 = (bf16[32,256]{1,0:T(8,128)(2,1)S(1)}, bf16[32,256]{1,0:T(8,128)(2,1)S(1)}, u32[]{:S(2)}, u32[]{:S(2)}) collective-permute-start(bf16[32,256]{1,0:T(8,128)(2,1)S(1)} %get-tuple-element.81), channel_id=1, source_target_pairs={{0,8},{8,16},{16,24},{24,0},{1,9},{9,17},{17,25},{25,1},{2,10},{10... | collective-permute-start | bytes 49160 | tf_op jit(solution)/shard_map/ppermute | solution.py:275
  79.7 5.2 %collective-permute-start.22 = (bf16[32,256]{1,0:T(8,128)(2,1)S(1)}, bf16[32,256]{1,0:T(8,128)(2,1)S(1)}, u32[]{:S(2)}, u32[]{:S(2)}) collective-permute-start(bf16[32,256]{1,0:T(8,128)(2,1)S(1)} %get-tuple-element.82), channel_id=1, source_target_pairs={{0,16},{8,24},{16,0},{24,8},{1,17},{9,25},{17,1},{25,9},{2,18},{10... | collective-permute-start | bytes 49160 | tf_op jit(solution)/shard_map/ppermute | solution.py:275
  81.1 3.8 %copy-start.14 = (bf16[32,256]{1,0:T(8,128)(2,1)}, bf16[32,256]{1,0:T(8,128)(2,1)S(1)}, u32[]{:S(2)}) copy-start(bf16[32,256]{1,0:T(8,128)(2,1)S(1)} %collective-permute-done.23.refs_3_) | copy-start | bytes 49156
  81.1 5.2 %collective-permute-start.21 = (bf16[32,256]{1,0:T(8,128)(2,1)S(1)}, bf16[32,256]{1,0:T(8,128)(2,1)S(1)}, u32[]{:S(2)}, u32[]{:S(2)}) collective-permute-start(bf16[32,256]{1,0:T(8,128)(2,1)S(1)} %get-tuple-element.83), channel_id=1, source_target_pairs={{0,24},{8,0},{16,8},{24,16},{1,25},{9,1},{17,9},{25,17},{2,26},{10... | collective-permute-start | bytes 49160 | tf_op jit(solution)/shard_map/ppermute | solution.py:275
  84.9 1.4 %copy-start.15 = (bf16[32,256]{1,0:T(8,128)(2,1)}, bf16[32,256]{1,0:T(8,128)(2,1)S(1)}, u32[]{:S(2)}) copy-start(bf16[32,256]{1,0:T(8,128)(2,1)S(1)} %collective-permute-done.22.refs_2_) | copy-start | bytes 49156
  84.9 5.9 %collective-permute-start.14 = (bf16[128,640]{1,0:T(8,128)(2,1)}, bf16[128,640]{1,0:T(8,128)(2,1)S(1)}, u32[]{:S(2)}, u32[]{:S(2)}) collective-permute-start(bf16[128,640]{1,0:T(8,128)(2,1)} %get-tuple-element.53), channel_id=1, source_target_pairs={{0,8},{8,16},{16,24},{24,0},{1,9},{9,17},{17,25},{25,1},{2,10},{10... | collective-permute-start | bytes 491528 | tf_op jit(solution)/shard_map/ppermute | solution.py:275
  86.3 0.6 copy-start.16
  86.9 3.9 %copy-start.2 = (bf16[128,640]{1,0:T(8,128)(2,1)S(1)}, bf16[128,640]{1,0:T(8,128)(2,1)}, u32[]{:S(2)}) copy-start(bf16[128,640]{1,0:T(8,128)(2,1)} %copy-done.1) | copy-start | bytes 491524
  86.9 1.2 collective-permute-start.24
  88.2 1.2 copy-start.17
  88.2 8.8 %collective-permute-start.15 = (bf16[128,640]{1,0:T(8,128)(2,1)}, bf16[128,640]{1,0:T(8,128)(2,1)S(1)}, u32[]{:S(2)}, u32[]{:S(2)}) collective-permute-start(bf16[128,640]{1,0:T(8,128)(2,1)} %get-tuple-element.54), channel_id=1, source_target_pairs={{0,16},{8,24},{16,0},{24,8},{1,17},{9,25},{17,1},{25,9},{2,18},{10... | collective-permute-start | bytes 491528 | tf_op jit(solution)/shard_map/ppermute | solution.py:275
  90.8 6.1 %copy-start.4 = (bf16[128,640]{1,0:T(8,128)(2,1)}, bf16[128,640]{1,0:T(8,128)(2,1)S(1)}, u32[]{:S(2)}) copy-start(bf16[128,640]{1,0:T(8,128)(2,1)S(1)} %collective-permute-done.14.refs_1_) | copy-start | bytes 491524
  90.8 29.8 %collective-permute-start.16 = (bf16[128,640]{1,0:T(8,128)(2,1)S(1)}, bf16[128,640]{1,0:T(8,128)(2,1)S(1)}, u32[]{:S(2)}, u32[]{:S(2)}) collective-permute-start(bf16[128,640]{1,0:T(8,128)(2,1)S(1)} %copy-done.2), channel_id=1, source_target_pairs={{0,24},{8,0},{16,8},{24,16},{1,25},{9,1},{17,9},{25,17},{2,26},{10... | collective-permute-start | bytes 491528 | tf_op jit(solution)/shard_map/ppermute | solution.py:275
  96.9 0.7 copy-start.5
  97.6 1.9 %copy-start.8 = (f32[16,1024]{1,0:T(8,128)S(1)}, f32[16,1024]{1,0:T(8,128)}, u32[]{:S(2)}) copy-start(f32[16,1024]{1,0:T(8,128)} %unpack_prompt.1) | copy-start | bytes 196612
  98.2 21.2 %collective-permute-start.27 = (bf16[128,256]{1,0:T(8,128)(2,1)S(1)}, bf16[128,256]{1,0:T(8,128)(2,1)S(1)}, u32[]{:S(2)}, u32[]{:S(2)}) collective-permute-start(bf16[128,256]{1,0:T(8,128)(2,1)S(1)} %get-tuple-element.77), channel_id=1, source_target_pairs={{0,8},{8,16},{16,24},{24,0},{1,9},{9,17},{17,25},{25,1},{2,10},{10... | collective-permute-start | bytes 196616 | tf_op jit(solution)/shard_map/ppermute | solution.py:275
  99.5 8.4 %collective-permute-start.29 = (f32[16,1024]{1,0:T(8,128)S(1)}, f32[16,1024]{1,0:T(8,128)S(1)}, u32[]{:S(2)}, u32[]{:S(2)}) collective-permute-start(f32[16,1024]{1,0:T(8,128)S(1)} %copy-done.8), channel_id=1, source_target_pairs={{0,32},{32,0},{64,96},{96,64},{128,160},{160,128},{192,224},{224,1... | collective-permute-start | bytes 196616 | tf_op jit(solution)/shard_map/ppermute | solution.py:328
  99.5 19.9 %collective-permute-start.26 = (bf16[128,256]{1,0:T(8,128)(2,1)S(1)}, bf16[128,256]{1,0:T(8,128)(2,1)S(1)}, u32[]{:S(2)}, u32[]{:S(2)}) collective-permute-start(bf16[128,256]{1,0:T(8,128)(2,1)S(1)} %get-tuple-element.78), channel_id=1, source_target_pairs={{0,16},{8,24},{16,0},{24,8},{1,17},{9,25},{17,1},{25,9},{2,18},{10... | collective-permute-start | bytes 196616 | tf_op jit(solution)/shard_map/ppermute | solution.py:275
  100.2 19.8 %collective-permute-start.25 = (bf16[128,256]{1,0:T(8,128)(2,1)S(1)}, bf16[128,256]{1,0:T(8,128)(2,1)S(1)}, u32[]{:S(2)}, u32[]{:S(2)}) collective-permute-start(bf16[128,256]{1,0:T(8,128)(2,1)S(1)} %get-tuple-element.79), channel_id=1, source_target_pairs={{0,24},{8,0},{16,8},{24,16},{1,25},{9,1},{17,9},{25,17},{2,26},{10... | collective-permute-start | bytes 196616 | tf_op jit(solution)/shard_map/ppermute | solution.py:275
  107.8 13.8 %collective-permute-start.30 = (f32[16,1024]{1,0:T(8,128)S(1)}, f32[16,1024]{1,0:T(8,128)S(1)}, u32[]{:S(2)}, u32[]{:S(2)}) collective-permute-start(f32[16,1024]{1,0:T(8,128)S(1)} %add.38), channel_id=1, source_target_pairs={{0,64},{32,96},{64,0},{96,32},{128,192},{160,224},{192,128},{224,1... | collective-permute-start | bytes 196616 | tf_op jit(solution)/shard_map/ppermute | solution.py:328
  119.4 0.6 copy-start.10
  119.4 0.6 copy-start.11
  120.0 0.6 copy-start.12
  120.6 1.3 %collective-permute-start.28 = (bf16[4,64,256]{2,1,0:T(8,128)(2,1)S(1)}, bf16[4,64,256]{2,1,0:T(8,128)(2,1)S(1)}, u32[]{:S(2)}, u32[]{:S(2)}) collective-permute-start(bf16[4,64,256]{2,1,0:T(8,128)(2,1)S(1)} %pad_maximum_fusion.6), channel_id=1, source_target_pairs={{0,1},{1,0},{2,3},{3,2},{4,5},{5,4},{6,7},{7,6},{8,9},{9,8},{10,11... | collective-permute-start | bytes 393224 | tf_op jit(solution)/shard_map/ppermute | solution.py:279
  120.6 1.0 copy-start.6
  121.7 5.9 %collective-permute-start.31 = (f32[16,1024]{1,0:T(8,128)S(1)}, f32[16,1024]{1,0:T(8,128)S(1)}, u32[]{:S(2)}, u32[]{:S(2)}) collective-permute-start(f32[16,1024]{1,0:T(8,128)S(1)} %add.39), channel_id=1, source_target_pairs={{0,128},{32,160},{64,192},{96,224},{128,0},{160,32},{192,64},{224,... | collective-permute-start | bytes 196616 | tf_op jit(solution)/shard_map/ppermute | solution.py:328
  121.8 6.3 %collective-permute-start.17 = (bf16[4,64,640]{2,1,0:T(8,128)(2,1)S(1)}, bf16[4,64,640]{2,1,0:T(8,128)(2,1)S(1)}, u32[]{:S(2)}, u32[]{:S(2)}) collective-permute-start(bf16[4,64,640]{2,1,0:T(8,128)(2,1)S(1)} %pad_maximum_fusion.5), channel_id=1, source_target_pairs={{0,1},{1,0},{2,3},{3,2},{4,5},{5,4},{6,7},{7,6},{8,9},{9,8},{10,11... | collective-permute-start | bytes 983048 | tf_op jit(solution)/shard_map/ppermute | solution.py:279
  122.0 0.7 copy-start.13
  128.2 0.7 copy-start.7
